TPU v7x, 256 devices: a whole 4x4x8 slice. The times are simulated.
256 devices in a mesh: gx: 8 (over y, x_hi), gy: 8 (over z), gz: 4 (over x_lo, core).
Axes of the slice: x: 4 (x_hi: 2, x_lo: 2; x = x_hi * 2 + x_lo), y: 4, z: 8, core: 2. Of those that a mesh axis runs over, the one named last changes fastest.
Arguments:
- populations: float32 [19, 128, 128, 512], P(None, 'gx', 'gy', 'gz'), may hold values from 0.02 to 0.1
- solid_flags: int32 [128, 128, 512], P('gx', 'gy', 'gz'), may hold values 0 or 1
- positions: float32 [7168, 3, 128], P(('gx', 'gy', 'gz')), may hold values from -4 to 4
- anchors: float32 [7168, 3, 128], P(('gx', 'gy', 'gz')), may hold values from -4 to 4
- base_cell: int32 [7168, 3, 128], P(('gx', 'gy', 'gz')), may hold values from 0 to 510, as said below
- weights: float32 [7168, 8, 128], P(('gx', 'gy', 'gz')), may hold values from 0.1 to 0.2
- intersection: int32 [7168, 2], P(('gx', 'gy', 'gz')), may hold values from 0 to 31, as said below
Outputs:
- read: float32 [19, 128, 128, 512], P(None, 'gx', 'gy', 'gz')
- vertex_velocity: float32 [7168, 3, 128], P(('gx', 'gy', 'gz'))
Inputs may be any that keep to these rules, and one draw needn't show every extreme that they name: `intersection`: patch p's two bricks differ and lie in its owner's slab. For every owner, no brick is listed by more than 4 of its patches, and in every slab a quarter of the bricks are listed by exactly 4 patches of every owner of that slab. `base_cell`: all eight kernel cells of a vertex lie in one brick, in the slab of the patch's owner, and that brick is on the patch's list.
All inputs are finite; a program needn't handle non-finite values. No bound on the sum of `solid_flags` on one device may be relied on, other than what follows from the above.
Results may differ from a plain program's by a relative error of at most 0.00011.
Values sent between devices are 32-bit elements; how exact they have to be, the bound alone decides.
A program may use at most 320 MiB of HBM per device.

v0:
```python
import jax
import jax.numpy as jnp
from jax import lax
from jax.sharding import PartitionSpec as P

SLOT_CAP = 4


RELAXATION = 0.8
TENSION = 0.05
TETHER = 0.5
VELOCITIES = [
    (0, 0, 0),
    (1, 0, 0),
    (-1, 0, 0),
    (0, 1, 0),
    (0, -1, 0),
    (0, 0, 1),
    (0, 0, -1),
    (1, 1, 0),
    (-1, -1, 0),
    (1, -1, 0),
    (-1, 1, 0),
    (1, 0, 1),
    (-1, 0, -1),
    (1, 0, -1),
    (-1, 0, 1),
    (0, 1, 1),
    (0, -1, -1),
    (0, 1, -1),
    (0, -1, 1),
]
OPPOSITE = [0, 2, 1, 4, 3, 6, 5, 8, 7, 10, 9, 12, 11, 14, 13, 16, 15, 18, 17]
LATTICE_WEIGHTS = [1.0 / 3.0] + [1.0 / 18.0] * 6 + [1.0 / 36.0] * 12


def extended(cells, sides, width):
    for axis, dim in sides:
        count = lax.axis_size(axis)
        head = lax.slice_in_dim(cells, 0, width, axis=dim)
        tail = lax.slice_in_dim(cells, cells.shape[dim] - width, cells.shape[dim], axis=dim)
        cells = jnp.concatenate(
            [
                lax.ppermute(tail, axis, [(i, (i + 1) % count) for i in range(count)]),
                cells,
                lax.ppermute(head, axis, [((i + 1) % count, i) for i in range(count)]),
            ],
            axis=dim,
        )
    return cells


def membrane_force(positions, anchors):
    cycle_term = jnp.roll(positions, 1, axis=2) + jnp.roll(positions, -1, axis=2) - 2.0 * positions
    return TENSION * cycle_term + TETHER * (anchors - positions)


def collide(populations, solid_flags, force_field):
    lattice = jnp.asarray(VELOCITIES, jnp.float32)
    density = jnp.sum(populations, axis=0)
    momentum = jnp.einsum("qa,qxyz->axyz", lattice, populations, precision=lax.Precision.HIGHEST)
    velocity = (momentum + 0.5 * force_field) / density
    speed_sq = velocity[0] * velocity[0] + velocity[1] * velocity[1] + velocity[2] * velocity[2]
    u_dot_f = (
        velocity[0] * force_field[0] + velocity[1] * force_field[1] + velocity[2] * force_field[2]
    )
    factor = 1.0 - 0.5 / RELAXATION
    outputs = []
    for direction in range(19):
        move_x, move_y, move_z = VELOCITIES[direction]
        along_u = move_x * velocity[0] + move_y * velocity[1] + move_z * velocity[2]
        along_f = move_x * force_field[0] + move_y * force_field[1] + move_z * force_field[2]
        weight_q = LATTICE_WEIGHTS[direction]
        equilibrium = (
            weight_q * density * (1.0 + 3.0 * along_u + 4.5 * along_u * along_u - 1.5 * speed_sq)
        )
        forcing = factor * weight_q * (3.0 * (along_f - u_dot_f) + 9.0 * along_u * along_f)
        current = populations[direction]
        relaxed = current - (current - equilibrium) / RELAXATION + forcing
        outputs.append(jnp.where(solid_flags == 1, populations[OPPOSITE[direction]], relaxed))
    return (jnp.stack(outputs), velocity)


def kernel_cells(table_rows, listed, root, extent):
    cell_int = table_rows[:, 11:14, :].astype(jnp.int32)
    local_x = cell_int[:, 0, :] - root[0]
    local_y = cell_int[:, 1, :] - root[1]
    local_z = cell_int[:, 2, :] - root[2]
    inside = (
        (local_x >= 0)
        & (local_x < extent[0])
        & (local_y >= 0)
        & (local_y < extent[1])
        & (local_z >= 0)
        & (local_z < extent[2])
    )
    live_mask = inside.astype(jnp.float32) * listed[:, None]
    local_x = jnp.where(inside, local_x, 0)
    local_y = jnp.where(inside, local_y, 0)
    local_z = jnp.where(inside, local_z, 0)
    index_list = []
    weight_list = []
    for corner in range(8):
        offset_x = corner >> 2 & 1
        offset_y = corner >> 1 & 1
        offset_z = corner & 1
        index_list.append(
            ((local_x + offset_x) * extent[1] + local_y + offset_y) * extent[2] + local_z + offset_z
        )
        weight_list.append(table_rows[:, 3 + corner, :] * live_mask)
    return (jnp.stack(index_list), jnp.stack(weight_list))


def fluid_update(populations, solid_flags, table_rows, listed, root):
    extent = populations.shape[1:]
    row_count = table_rows.shape[0]
    count_v = table_rows.shape[2]
    block_rows = row_count
    while block_rows > 256 and block_rows % 2 == 0:
        block_rows = block_rows // 2
    block_count = row_count // block_rows
    cell_index, kernel = kernel_cells(table_rows, listed, root, extent)
    index_blocks = jnp.transpose(
        cell_index.reshape(8, block_count, block_rows, count_v), (1, 0, 2, 3)
    )
    kernel_blocks = jnp.transpose(kernel.reshape(8, block_count, block_rows, count_v), (1, 0, 2, 3))
    force_blocks = table_rows[:, 0:3, :].reshape(block_count, block_rows, 3, count_v)
    cell_total = extent[0] * extent[1] * extent[2]

    def spread(total, block):
        index_part, kernel_part, force_part = block
        contrib = kernel_part[:, :, None, :] * force_part[None]
        contrib = jnp.transpose(contrib, (2, 0, 1, 3)).reshape(3, -1)
        return (total.at[:, index_part.reshape(-1)].add(contrib), None)

    force_field, _ = lax.scan(
        spread, jnp.zeros((3, cell_total), jnp.float32), (index_blocks, kernel_blocks, force_blocks)
    )
    post_collision, velocity = collide(
        populations, solid_flags, force_field.reshape(3, extent[0], extent[1], extent[2])
    )
    flat_velocity = velocity.reshape(3, -1)

    def sample(carry, block):
        index_part, kernel_part = block
        picked = flat_velocity[:, index_part.reshape(-1)].reshape(3, 8, block_rows, count_v)
        summed = jnp.sum(picked * kernel_part[None], axis=1)
        return (carry, jnp.transpose(summed, (1, 0, 2)))

    _, sampled_sum = lax.scan(sample, jnp.zeros((), jnp.float32), (index_blocks, kernel_blocks))
    return (post_collision, sampled_sum.reshape(row_count, 3, count_v))


def body(populations, solid_flags, positions, anchors, base_cell, weights, intersection):
    patch_count = positions.shape[0]
    count_v = positions.shape[2]
    size_x, size_y, size_z = (populations.shape[1], populations.shape[2], populations.shape[3])
    bricks = lax.axis_size("gy") * lax.axis_size("gz")
    root = (
        lax.axis_index("gx") * size_x,
        lax.axis_index("gy") * size_y,
        lax.axis_index("gz") * size_z,
    )
    forces = membrane_force(positions, anchors)
    payload = jnp.concatenate([forces, weights, base_cell.astype(jnp.float32)], axis=1)
    entries = intersection.reshape(-1)
    onehot = (entries[:, None] == jnp.arange(bricks, dtype=jnp.int32)[None, :]).astype(jnp.int32)
    slot_rank = jnp.sum(jnp.cumsum(onehot, axis=0) * onehot, axis=1) - 1
    slot_target = entries * SLOT_CAP + slot_rank
    entry_patch = jnp.arange(2 * patch_count, dtype=jnp.int32) // 2
    slot_patch = jnp.full((bricks * SLOT_CAP,), -1, jnp.int32).at[slot_target].set(entry_patch)
    slot_live = (slot_patch >= 0).astype(jnp.float32)
    outgoing = jnp.take(payload, jnp.maximum(slot_patch, 0), axis=0) * slot_live[:, None, None]
    outgoing = outgoing.reshape(bricks, SLOT_CAP, 14, count_v)
    received = lax.all_to_all(outgoing, ("gy", "gz"), split_axis=0, concat_axis=0, tiled=True)
    table_rows = received.reshape(bricks * SLOT_CAP, 14, count_v)
    listed = jnp.ones((bricks * SLOT_CAP,), jnp.float32)
    post_collision, sampled_sum = fluid_update(populations, solid_flags, table_rows, listed, root)
    returned = lax.all_to_all(
        sampled_sum.reshape(bricks, SLOT_CAP, 3, count_v),
        ("gy", "gz"),
        split_axis=0,
        concat_axis=0,
        tiled=True,
    )
    returned = returned.reshape(bricks * SLOT_CAP, 3, count_v)
    vertex_velocity = (
        jnp.take(returned, slot_target, axis=0).reshape(patch_count, 2, 3, count_v).sum(axis=1)
    )
    padded = extended(post_collision, (("gx", 1), ("gy", 2), ("gz", 3)), 1)
    read = jnp.stack(
        [
            padded[
                direction,
                1 - VELOCITIES[direction][0] : 1 - VELOCITIES[direction][0] + size_x,
                1 - VELOCITIES[direction][1] : 1 - VELOCITIES[direction][1] + size_y,
                1 - VELOCITIES[direction][2] : 1 - VELOCITIES[direction][2] + size_z,
            ]
            for direction in range(19)
        ]
    )
    return (read, vertex_velocity)


def solution(mesh):
    return jax.shard_map(
        body,
        mesh=mesh,
        in_specs=(
            P(None, "gx", "gy", "gz"),
            P("gx", "gy", "gz"),
            P(("gx", "gy", "gz"), None, None),
            P(("gx", "gy", "gz"), None, None),
            P(("gx", "gy", "gz"), None, None),
            P(("gx", "gy", "gz"), None, None),
            P(("gx", "gy", "gz"), None),
        ),
        out_specs=(P(None, "gx", "gy", "gz"), P(("gx", "gy", "gz"), None, None)),
        check_vma=False,
    )
```

profile of v0, /device:TPU:1, one launch (start us, length us, event | category | flops | bytes accessed | tf_op | source)
XLA Modules:
  0.0 1599.5 jit_solution(14793189572177685183)
XLA Ops:
  1.6 1.0 fusion.231
  9.9 1.1 copy.128
  11.0 11.1 all-to-all-start
  23.8 23.7 %all-to-all-done = f32[32,4,14,128]{3,1,2,0:T(4,128)} async-done(((f32[32,4,14,128]{3,1,2,0:T(4,128)}), f32[32,4,14,128]{3,1,2,0:T(4,128)}, u32[]{:S(2)}, u32[]{:S(2)}) %all-to-all-start) | async-done | bytes 917536 | tf_op jit(solution)/shard_map/all_to_all | solution.py:175
  47.5 1.4 copy.129
  50.0 1.4 compare_select_fusion
  51.4 5.6 copy.130
  62.9 44.1 %bitcast_multiply_fusion = f32[3,131072]{0,1:T(8,128)} fusion(f32[3,128,128]{0,2,1:T(8,128)} %copy.130, f32[131072]{0:T(1024)S(1)} %bitcast.396), kind=kLoop, calls=%fused_computation.7 | loop fusion | flops 393216 | bytes 2293760 | tf_op jit(solution)/shard_map/while/body/eval_jaxpr/mul | solution.py:132
  107.0 845.0 %scatter_custom_fusion.1 = f32[3,32768]{0,1:T(8,128)} fusion(s32[131072]{0:T(1024)} %bitcast.397, f32[3,131072]{0,1:T(8,128)} %bitcast_multiply_fusion, f32[]{:T(128)} %constant.144.clone.1), kind=kCustom, calls=%fused_computation.5 | custom fusion | flops 393216 | bytes 67502592 | tf_op jit(solution)/shard_map/while/body/eval_jaxpr/scatter-add | solution.py:134
  952.0 30.4 %slice_reduce_fusion.2 = (f32[32768]{0:T(1024)S(1)}, f32[32768]{0:T(1024)S(1)}, f32[32768]{0:T(1024)S(1)}) fusion(f32[3,32768]{0,1:T(8,128)} %scatter_custom_fusion.1), kind=kLoop, calls=%fused_computation.11 | loop fusion | bytes 786432 | tf_op jit(solution)/shard_map/slice | solution.py:72
  982.4 11.4 broadcast_multiply_fusion
  994.7 9.8 copy.148
  1004.6 4.1 fusion.8
  1009.2 1.5 copy.187
  1010.7 1.1 copy-done.2
  1015.6 2.4 collective-permute-start
  1018.0 2.7 collective-permute-start.1
  1020.7 9.0 copy.141
  1029.7 480.8 %gather_fusion.1 = f32[131072,3]{1,0:T(8,128)} fusion(f32[3,32768]{0,1:T(8,128)} %copy.141, s32[131072]{0:T(1024)} %broadcast_clamp_fusion), kind=kCustom, calls=%fused_computation.1 | custom fusion | bytes 3670016 | tf_op jit(solution)/shard_map/while/body/eval_jaxpr/gather | solution.py:146
  1510.4 25.9 %multiply_reduce_fusion = f32[3,128,128]{0,2,1:T(8,128)} fusion(f32[3,8,128,128]{0,3,2,1:T(8,128)} %bitcast.67, f32[8,128,128]{2,1,0:T(8,128)S(1)} %constant_dynamic-update-slice_fusion.8), kind=kLoop, calls=%fused_computation.8 | loop fusion | flops 737280 | bytes 2293760 | tf_op jit(solution)/shard_map/while/body/eval_jaxpr/reduce_sum | solution.py:147
  1536.3 5.9 copy.142
  1542.2 5.2 all-to-all-start.1
  1547.7 1.5 collective-permute-start.2
  1549.1 1.5 collective-permute-start.3
  1551.9 7.1 collective-permute-done.2
  1559.7 4.5 fusion.227
  1564.2 3.7 copy.135
  1567.9 2.0 collective-permute-start.4
  1569.9 4.3 copy.137
  1575.6 5.0 copy.136
  1580.6 5.0 copy.138
  1585.6 1.9 maximum_dynamic-update-slice_fusion.9
  (126 shorter events, 37.5 us)
Async XLA Ops:
  9.5 12.8 copy-start.8
  9.5 13.5 copy-start.1
  11.0 36.5 %all-to-all-start = ((f32[32,4,14,128]{3,1,2,0:T(4,128)}), f32[32,4,14,128]{3,1,2,0:T(4,128)}, u32[]{:S(2)}, u32[]{:S(2)}) async-start(f32[32,4,14,128]{3,1,2,0:T(4,128)} %copy.128), calls=%async_computation | async-start | bytes 1835008 | tf_op jit(solution)/shard_map/all_to_all | solution.py:175
  48.9 1.1 copy-start.3
  982.4 11.4 copy-start.4
  994.7 9.8 copy-start.9
  1004.6 4.4 copy-start.6
  1008.7 2.0 copy-start.5
  1009.2 2.6 copy-start.2
  1015.6 531.8 %collective-permute-start = (f32[19,1,16,128]{3,2,1,0:T(8,128)}, f32[19,1,16,128]{3,2,1,0:T(8,128)S(1)}, u32[]{:S(2)}, u32[]{:S(2)}) collective-permute-start(f32[19,1,16,128]{3,2,1,0:T(8,128)} %get-tuple-element.58), channel_id=1, source_target_pairs={{0,32},{32,64},{64,96},{96,128},{128,160},{160,192},{192,224},{224... | collective-permute-start | bytes 466952 | tf_op jit(solution)/shard_map/ppermute | solution.py:44
  1018.0 529.4 %collective-permute-start.1 = (f32[19,1,16,128]{3,2,1,0:T(8,128)S(1)}, f32[19,1,16,128]{3,2,1,0:T(8,128)S(1)}, u32[]{:S(2)}, u32[]{:S(2)}) collective-permute-start(f32[19,1,16,128]{3,2,1,0:T(8,128)S(1)} %get-tuple-element.57), channel_id=1, source_target_pairs={{32,0},{64,32},{96,64},{128,96},{160,128},{192,160},{224,192},{0,2... | collective-permute-start | bytes 466952 | tf_op jit(solution)/shard_map/ppermute | solution.py:46
  1542.2 55.6 %all-to-all-start.1 = ((f32[32,4,3,128]{3,1,2,0:T(4,128)}), f32[32,4,3,128]{3,1,2,0:T(4,128)S(1)}, u32[]{:S(2)}, u32[]{:S(2)}) async-start(f32[32,4,3,128]{3,1,2,0:T(4,128)} %copy.142), calls=%async_computation.1 | async-start | bytes 393216 | tf_op jit(solution)/shard_map/all_to_all | solution.py:179
  1547.7 11.3 collective-permute-start.2
  1549.1 9.9 collective-permute-start.3
  1567.9 7.7 collective-permute-start.4
  1574.2 6.4 collective-permute-start.5
  1585.6 2.3 copy-start
  1587.9 3.5 slice-start
  1588.7 2.7 slice-start.1
  1597.0 1.6 copy-start.7
where the time goes:
time: 1610 us; the launch traced here: 1600 us
  other arithmetic  959 us (60%)
  local copies, waits for them, and re-layouts  578 us (36%)
  waiting for transfers between devices  30.8 us (2%)
  starting transfers between devices  26.3 us (2%)
    scatter-add x1, other arithmetic, spread(): return (total.at[:, index_part.reshape(-1)].add(contrib), None)  845 us
    gather x1, local copies, waits for them, and re-layouts, sample(): flat_velocity[:, index_part.reshape(-1)].reshape(3, 8, block_rows, count_v)  481 us
    mul x2, other arithmetic, spread(): contrib = kernel_part[:, :, None, :] * force_part[None]  44.9 us
  transfers between devices with their start and end apart: 8, of which 2 were waited for; matrix products, arithmetic and copies ran while one was open for 35% of the time, Pallas kernels for 0%

commit v1 on v0

v1 whole, which is shorter than its diff:
```python
import jax
import jax.numpy as jnp
from jax import lax
from jax.experimental import pallas as pl
from jax.experimental.pallas import tpu as pltpu
from jax.sharding import PartitionSpec as P

SLOT_CAP = 4
VERT = 128
BRICKS = 32
PATCH_DEV = 28
ROWS = 56
HALF = 9 * 16

RELAXATION = 0.8
TENSION = 0.05
TETHER = 0.5
VELOCITIES = [
    (0, 0, 0),
    (1, 0, 0),
    (-1, 0, 0),
    (0, 1, 0),
    (0, -1, 0),
    (0, 0, 1),
    (0, 0, -1),
    (1, 1, 0),
    (-1, -1, 0),
    (1, -1, 0),
    (-1, 1, 0),
    (1, 0, 1),
    (-1, 0, -1),
    (1, 0, -1),
    (-1, 0, 1),
    (0, 1, 1),
    (0, -1, -1),
    (0, 1, -1),
    (0, -1, 1),
]
OPPOSITE = [0, 2, 1, 4, 3, 6, 5, 8, 7, 10, 9, 12, 11, 14, 13, 16, 15, 18, 17]
LATTICE_WEIGHTS = [1.0 / 3.0] + [1.0 / 18.0] * 6 + [1.0 / 36.0] * 12
F32 = jnp.float32
BF16 = jnp.bfloat16
OUTSIDE = -100.0


def prep_kernel(inter_ref, pos_ref, anc_ref, cell_ref, w_ref, out_ref, tgt_ref, count_ref):
    root_x = lax.axis_index("gx") * 16

    def clear_count(b, carry):
        count_ref[b] = 0
        return carry

    lax.fori_loop(0, BRICKS, clear_count, 0)

    def clear(b, carry):
        out_ref[b, 0:44] = jnp.zeros((44, VERT), F32)
        out_ref[b, 44:56] = jnp.full((12, VERT), OUTSIDE, F32)
        return carry

    lax.fori_loop(0, BRICKS, clear, 0)

    def patch(p, carry):
        pos = pos_ref[p]
        cycle = pltpu.roll(pos, 1, 1) + pltpu.roll(pos, VERT - 1, 1) - 2.0 * pos
        force = TENSION * cycle + TETHER * (anc_ref[p] - pos)
        cell = cell_ref[p]
        weight = w_ref[p]
        for j in range(2):
            b = inter_ref[p, j]
            r = count_ref[b]
            count_ref[b] = r + 1
            tgt_ref[p, j] = b * SLOT_CAP + r
            x = cell[0:1] - root_x
            y = cell[1:2] - (b // 4) * 16
            z = cell[2:3] - (b % 4) * 128
            inside = (x >= 0) & (x < 16) & (y >= 0) & (y < 16) & (z >= 0) & (z < 128)
            out_ref[b, pl.ds(pl.multiple_of(r * 8, 8), 8)] = weight
            for a, coord in enumerate((x, y, z)):
                out_ref[b, pl.ds(32 + 4 * a + r, 1)] = force[a : a + 1]
                out_ref[b, pl.ds(44 + 4 * a + r, 1)] = jnp.where(
                    inside, coord.astype(F32), OUTSIDE
                )
        return carry

    lax.fori_loop(0, PATCH_DEV, patch, 0)


def prep(intersection, positions, anchors, base_cell, weights):
    vmem = pl.BlockSpec(memory_space=pltpu.VMEM)
    smem = pl.BlockSpec(memory_space=pltpu.SMEM)
    return pl.pallas_call(
        prep_kernel,
        name="prep",
        out_shape=(
            jax.ShapeDtypeStruct((BRICKS, ROWS, VERT), F32),
            jax.ShapeDtypeStruct((PATCH_DEV, 2), jnp.int32),
        ),
        in_specs=[smem, vmem, vmem, vmem, vmem],
        out_specs=(vmem, smem),
        scratch_shapes=[pltpu.SMEM((BRICKS,), jnp.int32)],
    )(intersection, positions, anchors, base_cell, weights)


def halves(value):
    high = value.astype(BF16)
    return high, (value - high.astype(F32)).astype(BF16)


def scatter_chunk(tab_ref, i, a_ref, z_ref, acc_ref):
    y_iota = lax.broadcasted_iota(jnp.int32, (16, VERT), 0).astype(F32)
    z_iota = lax.broadcasted_iota(jnp.int32, (256, VERT), 0).astype(F32)
    zero16 = jnp.zeros((16, VERT), BF16)
    for s in range(SLOT_CAP):
        x = tab_ref[i, pl.ds(44 + s, 1)]
        y = tab_ref[i, pl.ds(48 + s, 1)]
        z = tab_ref[i, pl.ds(52 + s, 1)]
        upper = x >= 8.0
        x_in = jnp.where(upper, x - 8.0, x)
        column = jnp.where(upper, z + 128.0, z)
        lanes = slice(s * VERT, (s + 1) * VERT)
        z_ref[:, lanes] = jnp.where(z_iota == column, 1.0, 0.0).astype(BF16)
        at_y = y_iota == y
        at_y1 = y_iota - 1.0 == y
        x_wide = jnp.broadcast_to(x_in, (16, VERT)).astype(BF16)
        masks = [x_wide == jnp.asarray(k, BF16) for k in range(-1, 9)]
        for kz in range(2):
            for c in range(3):
                force = tab_ref[i, pl.ds(32 + 4 * c + s, 1)]
                parts = []
                for kx in range(2):
                    w0 = tab_ref[i, pl.ds(8 * s + 4 * kx + kz, 1)] * force
                    w1 = tab_ref[i, pl.ds(8 * s + 4 * kx + 2 + kz, 1)] * force
                    parts.append(halves(jnp.where(at_y, w0, jnp.where(at_y1, w1, 0.0))))
                base = (kz * 3 + c) * HALF
                for hl in range(2):
                    col = slice(hl * 512 + s * VERT, hl * 512 + (s + 1) * VERT)
                    for plane in range(9):
                        a_ref[base + plane * 16 : base + plane * 16 + 16, col] = jnp.where(
                            masks[plane + 1],
                            parts[0][hl],
                            jnp.where(masks[plane], parts[1][hl], zero16),
                        )
    zz = z_ref[...]
    for block in range(6):
        rows = slice(block * HALF, (block + 1) * HALF)
        dims = (((1,), (1,)), ((), ()))
        acc_ref[rows] += lax.dot_general(
            a_ref[rows, 0:512], zz, dims, preferred_element_type=F32
        ) + lax.dot_general(a_ref[rows, 512:1024], zz, dims, preferred_element_type=F32)


def finish_force(acc_ref, force_ref):
    for c in range(3):
        for plane in range(16):
            pair = []
            for kz in range(2):
                base = (kz * 3 + c) * HALF
                if plane < 8:
                    total = acc_ref[base + plane * 16 : base + plane * 16 + 16, 0:128]
                elif plane == 8:
                    total = (
                        acc_ref[base + 128 : base + 144, 0:128]
                        + acc_ref[base : base + 16, 128:256]
                    )
                else:
                    start = base + (plane - 8) * 16
                    total = acc_ref[start : start + 16, 128:256]
                pair.append(total)
            force_ref[c, plane * 16 : plane * 16 + 16] = pair[0] + pltpu.roll(pair[1], 1, 1)


def collide_all(pop_ref, solid_ref, force_ref, post_ref, vel_ref):
    factor = 1.0 - 0.5 / RELAXATION

    def chunk(step, carry):
        x = step // 2
        yy = pl.ds(pl.multiple_of((step % 2) * 8, 8), 8)
        rows = pl.ds(pl.multiple_of(step * 8, 8), 8)
        pops = [pop_ref[q, x, yy] for q in range(19)]
        solid = solid_ref[x, yy] == 1
        force = [force_ref[c, rows] for c in range(3)]
        density = sum(pops[1:], pops[0])
        inverse = 1.0 / density
        velocity = []
        for a in range(3):
            plus = [pops[q] for q in range(19) if VELOCITIES[q][a] == 1]
            minus = [pops[q] for q in range(19) if VELOCITIES[q][a] == -1]
            momentum = sum(plus[1:], plus[0]) - sum(minus[1:], minus[0])
            u = (momentum + 0.5 * force[a]) * inverse
            velocity.append(u)
            vel_ref[a, rows] = u
        speed_sq = velocity[0] * velocity[0] + velocity[1] * velocity[1] + velocity[2] * velocity[2]
        u_dot_f = velocity[0] * force[0] + velocity[1] * force[1] + velocity[2] * force[2]
        common = 1.0 - 1.5 * speed_sq

        def along(direction, parts):
            total = None
            for step_a, part in zip(direction, parts):
                if step_a:
                    term = part if step_a == 1 else -part
                    total = term if total is None else total + term
            return total

        for q in range(19):
            w = LATTICE_WEIGHTS[q]
            if q == 0:
                equilibrium = w * density * common
                forcing = (factor * w) * (-3.0 * u_dot_f)
            else:
                along_u = along(VELOCITIES[q], velocity)
                along_f = along(VELOCITIES[q], force)
                equilibrium = w * density * (common + along_u * (3.0 + 4.5 * along_u))
                forcing = (factor * w) * (3.0 * (along_f - u_dot_f) + 9.0 * along_u * along_f)
            relaxed = pops[q] - (pops[q] - equilibrium) * (1.0 / RELAXATION) + forcing
            post_ref[q, x, yy] = jnp.where(solid, pops[OPPOSITE[q]], relaxed)
        return carry

    lax.fori_loop(0, 32, chunk, 0)


def transpose_velocity(vel_ref, vt_ref):
    for c in range(3):
        high, low = halves(vel_ref[c].T)
        rows = slice(c * 128, (c + 1) * 128)
        vt_ref[rows, 0:256] = high
        vt_ref[rows, 256:512] = high
        vt_ref[rows, 512:768] = low


def gather_chunk(tab_ref, i, b_ref, vt_ref, ret_ref):
    y_iota = lax.broadcasted_iota(jnp.int32, (16, VERT), 0).astype(F32)
    z_iota = lax.broadcasted_iota(jnp.int32, (VERT, VERT), 0).astype(F32)
    zero16 = jnp.zeros((16, VERT), BF16)
    for s in range(SLOT_CAP):
        x = tab_ref[i, pl.ds(44 + s, 1)]
        y = tab_ref[i, pl.ds(48 + s, 1)]
        z = tab_ref[i, pl.ds(52 + s, 1)]
        at_y = y_iota == y
        at_y1 = y_iota - 1.0 == y
        x_wide = jnp.broadcast_to(x, (16, VERT)).astype(BF16)
        masks = [x_wide == jnp.asarray(k, BF16) for k in range(-1, 16)]
        for kz in range(2):
            parts = []
            for kx in range(2):
                w0 = tab_ref[i, pl.ds(8 * s + 4 * kx + kz, 1)]
                w1 = tab_ref[i, pl.ds(8 * s + 4 * kx + 2 + kz, 1)]
                parts.append(halves(jnp.where(at_y, w0, jnp.where(at_y1, w1, 0.0))))
            cols = slice(kz * VERT, (kz + 1) * VERT)
            for hl in range(2):
                for plane in range(16):
                    value = jnp.where(
                        masks[plane + 1],
                        parts[0][hl],
                        jnp.where(masks[plane], parts[1][hl], zero16),
                    )
                    row = hl * 256 + plane * 16
                    b_ref[s, row : row + 16, cols] = value
                    if hl == 0:
                        b_ref[s, 512 + plane * 16 : 528 + plane * 16, cols] = value
        picked = jnp.dot(vt_ref[...], b_ref[s], preferred_element_type=F32)
        at_z = z_iota == z
        at_z1 = z_iota - 1.0 == z
        for c in range(3):
            rows = slice(c * 128, (c + 1) * 128)
            both = jnp.where(at_z, picked[rows, 0:128], 0.0) + jnp.where(
                at_z1, picked[rows, 128:256], 0.0
            )
            ret_ref[i, pl.ds(4 * c + s, 1)] = jnp.sum(both, axis=0, keepdims=True)


def core_kernel(
    tab_ref, pop_ref, solid_ref, post_ref, ret_ref, a_ref, z_ref, acc_ref, force_ref, vel_ref, vt_ref, b_ref
):
    acc_ref[...] = jnp.zeros_like(acc_ref)

    def scatter(i, carry):
        scatter_chunk(tab_ref, i, a_ref, z_ref, acc_ref)
        return carry

    lax.fori_loop(0, BRICKS, scatter, 0)
    finish_force(acc_ref, force_ref)
    collide_all(pop_ref, solid_ref, force_ref, post_ref, vel_ref)
    transpose_velocity(vel_ref, vt_ref)

    def gather(i, carry):
        gather_chunk(tab_ref, i, b_ref, vt_ref, ret_ref)
        return carry

    lax.fori_loop(0, BRICKS, gather, 0)


def core(table, populations, solid_flags):
    vmem = pl.BlockSpec(memory_space=pltpu.VMEM)
    return pl.pallas_call(
        core_kernel,
        name="core",
        out_shape=(
            jax.ShapeDtypeStruct(populations.shape, F32),
            jax.ShapeDtypeStruct((BRICKS, 12, VERT), F32),
        ),
        in_specs=[vmem] * 3,
        out_specs=(vmem, vmem),
        scratch_shapes=[
            pltpu.VMEM((6 * HALF, 1024), BF16),
            pltpu.VMEM((256, 512), BF16),
            pltpu.VMEM((6 * HALF, 256), F32),
            pltpu.VMEM((3, 256, 128), F32),
            pltpu.VMEM((3, 256, 128), F32),
            pltpu.VMEM((384, 768), BF16),
            pltpu.VMEM((4, 768, 256), BF16),
        ],
        compiler_params=pltpu.CompilerParams(vmem_limit_bytes=32 * 1024 * 1024),
    )(table, populations, solid_flags)


def combine_kernel(tgt_ref, returned_ref, out_ref):
    def patch(p, carry):
        first, second = tgt_ref[p, 0], tgt_ref[p, 1]
        for c in range(3):
            out_ref[p, c : c + 1] = (
                returned_ref[first // SLOT_CAP, pl.ds(4 * c + first % SLOT_CAP, 1)]
                + returned_ref[second // SLOT_CAP, pl.ds(4 * c + second % SLOT_CAP, 1)]
            )
        return carry

    lax.fori_loop(0, PATCH_DEV, patch, 0)


def combine(target, returned):
    vmem = pl.BlockSpec(memory_space=pltpu.VMEM)
    return pl.pallas_call(
        combine_kernel,
        name="combine",
        out_shape=jax.ShapeDtypeStruct((PATCH_DEV, 3, VERT), F32),
        in_specs=[pl.BlockSpec(memory_space=pltpu.SMEM), vmem],
        out_specs=vmem,
    )(target, returned)


def stream(post):
    lists = [post[q] for q in range(19)]
    for dim, axis in enumerate(("gx", "gy", "gz")):
        plus = [q for q in range(19) if VELOCITIES[q][dim] == 1]
        minus = [q for q in range(19) if VELOCITIES[q][dim] == -1]
        size = lists[0].shape[dim]
        count = lax.axis_size(axis)
        up = jnp.stack([lax.slice_in_dim(lists[q], size - 1, size, axis=dim) for q in plus])
        down = jnp.stack([lax.slice_in_dim(lists[q], 0, 1, axis=dim) for q in minus])
        before = lax.ppermute(up, axis, [(i, (i + 1) % count) for i in range(count)])
        after = lax.ppermute(down, axis, [((i + 1) % count, i) for i in range(count)])
        for k, q in enumerate(plus):
            body = lax.slice_in_dim(lists[q], 0, size - 1, axis=dim)
            lists[q] = jnp.concatenate([before[k], body], axis=dim)
        for k, q in enumerate(minus):
            body = lax.slice_in_dim(lists[q], 1, size, axis=dim)
            lists[q] = jnp.concatenate([body, after[k]], axis=dim)
    return jnp.stack(lists)


def body(populations, solid_flags, positions, anchors, base_cell, weights, intersection):
    outgoing, target = prep(intersection, positions, anchors, base_cell, weights)
    table = lax.all_to_all(outgoing, ("gy", "gz"), split_axis=0, concat_axis=0, tiled=True)
    post, summed = core(table, populations, solid_flags)
    returned = lax.all_to_all(summed, ("gy", "gz"), split_axis=0, concat_axis=0, tiled=True)
    vertex_velocity = combine(target, returned)
    return (stream(post), vertex_velocity)


def solution(mesh):
    return jax.shard_map(
        body,
        mesh=mesh,
        in_specs=(
            P(None, "gx", "gy", "gz"),
            P("gx", "gy", "gz"),
            P(("gx", "gy", "gz"), None, None),
            P(("gx", "gy", "gz"), None, None),
            P(("gx", "gy", "gz"), None, None),
            P(("gx", "gy", "gz"), None, None),
            P(("gx", "gy", "gz"), None),
        ),
        out_specs=(P(None, "gx", "gy", "gz"), P(("gx", "gy", "gz"), None, None)),
        check_vma=False,
    )
```

time: 1610 us -> 164 us (0.10)
  other arithmetic: 959 us -> 9.6 us
  local copies, waits for them, and re-layouts: 578 us -> 18.6 us
  Pallas kernels: 0 us -> 78.5 us
  blocking collectives: 0 us -> 36.4 us
  waiting for transfers between devices: 30.8 us -> 5.28 us
    scatter-add x1 -> x0, other arithmetic: 845 us -> none  [spread(): return (total.at[:, index_part.reshape(-1)].add(contrib), None)]
    gather x4 -> x0, local copies, waits for them, and re-layouts: 483 us -> none  [the longest x1 481 us: sample(): flat_velocity[:, index_part.reshape(-1)].reshape(3, 8, block_rows, count_v)]
    pallas_call x0 -> x3, Pallas kernels: none -> 78.5 us  [the longest x1 71.8 us: core(): pl.pallas_call(core_kernel, name='core', out_shape=(jax.ShapeDtypeStruct(...]
    mul x5 -> x0, other arithmetic: 57.3 us -> none  [the longest x2 44.9 us: spread(): contrib = kernel_part[:, :, None, :] * force_part[None]]
    slice x8 -> x13, local copies, waits for them, and re-layouts: 45.8 us -> 0.76 us  [the longest x2 0.28 us: stream(): lax.slice_in_dim(lists[q], 0, 1, axis=dim)]
    all_to_all x0 -> x1, blocking collectives: none -> 36.4 us  [body(): lax.all_to_all(outgoing, ('gy', 'gz'), split_axis=0, concat_axis=0, tiled...]
    reduce_sum x4 -> x0, other arithmetic: 26.4 us -> none  [the longest x1 25.9 us: sample(): summed = jnp.sum(picked * kernel_part[None], axis=1)]
    all_to_all x2 -> x1, waiting for transfers between devices: 23.7 us -> 0.01 us  [body(): lax.all_to_all(summed, ('gy', 'gz'), split_axis=0, concat_axis=0, tiled=T...]
  transfers between devices with their start and end apart: 8 -> 7, of which waited for: 2 -> 3; matrix products, arithmetic and copies ran while one was open for 35% -> 10% of each run, Pallas kernels for 0% -> 0%
where the time goes in v1:
time: 164 us
  Pallas kernels  78.5 us (48%)
  blocking collectives  36.4 us (22%)
  local copies, waits for them, and re-layouts  18.6 us (11%)
  starting transfers between devices  14.3 us (9%)
  other arithmetic  9.6 us (6%)
  waiting for transfers between devices  5.28 us (3%)
    pallas_call x1, Pallas kernels, core(): pl.pallas_call(core_kernel, name='core', out_shape=(jax.ShapeDtypeStruct(...  71.8 us
    all_to_all x1, blocking collectives, body(): lax.all_to_all(outgoing, ('gy', 'gz'), split_axis=0, concat_axis=0, tiled...  36.4 us
    unnamed x34, local copies, waits for them, and re-layouts  14.5 us
    ppermute x3, starting transfers between devices, stream(): lax.ppermute(down, axis, [((i + 1) % count, i) for i in range(count)])  8.08 us
    unnamed x13, other arithmetic  7.57 us
    all_to_all x1, starting transfers between devices, body(): lax.all_to_all(summed, ('gy', 'gz'), split_axis=0, concat_axis=0, tiled=T...  4.98 us
    pallas_call x1, Pallas kernels, prep(): pl.pallas_call(prep_kernel, name='prep', out_shape=(jax.ShapeDtypeStruct(...  4.57 us
    ppermute x3, waiting for transfers between devices, stream(): lax.ppermute(down, axis, [((i + 1) % count, i) for i in range(count)])  3.85 us
  transfers between devices with their start and end apart: 7, of which 3 were waited for; matrix products, arithmetic and copies ran while one was open for 10% of the time, Pallas kernels for 0%

profile of v1, /device:TPU:1, one launch (start us, length us, event | category | flops | bytes accessed | tf_op | source)
XLA Modules:
  0.0 163.7 jit_solution(14415753374158199742)
XLA Ops:
  0.6 1.5 copy.525.pos_ref
  2.1 1.4 copy.526.anc_ref
  3.6 1.4 copy.527.cell_ref
  5.0 1.4 copy.524.inter_ref
  6.4 4.6 %prep.1 = (f32[32,56,128]{2,1,0:T(8,128)}, s32[28,2]{1,0:T(8,128)}) custom-call(s32[28,2]{1,0:T(8,128)} %copy.524.inter_ref, f32[28,3,128]{2,1,0:T(4,128)} %copy.525.pos_ref, f32[28,3,128]{2,1,0:T(4,128)} %copy.526.anc_ref, s32[28,3,128]{2,1,0:T(4,128)} %copy.527.cell_ref, f32[28,8,128]{2,1,0:T(8,128)} %w_ref.1), custom_call_target="tpu_custom_call" | custom-call | tf_op jit(solution)/shard_map/prep/pallas_call | solution.py:91
  11.0 36.4 %all_to_all.10.tab_ref = f32[32,56,128]{2,1,0:T(8,128)S(1)} all-to-all(f32[32,56,128]{2,1,0:T(8,128)} %get-tuple-element.6), channel_id=1, replica_groups=mesh['gx'=8,'gy'=8,'gz'=4] {'gy','gz'}, dimensions={0} | all-to-all | bytes 1835008 | tf_op jit(solution)/shard_map/all_to_all | solution.py:362
  47.4 1.7 %copy-done = f32[19,16,16,128]{3,2,1,0:T(8,128)S(1)} copy-done((f32[19,16,16,128]{3,2,1,0:T(8,128)S(1)}, f32[19,16,16,128]{3,2,1,0:T(8,128)}, u32[]{:S(2)}) %copy-start) | copy-done | bytes 2490392
  49.1 71.8 %core.1 = (f32[19,16,16,128]{3,2,1,0:T(8,128)S(1)}, f32[32,12,128]{2,1,0:T(8,128)}) custom-call(f32[32,56,128]{2,1,0:T(8,128)S(1)} %all_to_all.10.tab_ref, f32[19,16,16,128]{3,2,1,0:T(8,128)S(1)} %copy-done, s32[16,16,128]{2,1,0:T(8,128)S(1)} %copy-done.1), custom_call_target="tpu_custom_call" | custom-call | tf_op jit(solution)/shard_map/core/pallas_call | solution.py:294
  120.9 0.9 copy.528
  121.9 0.7 slice_bitcast_fusion.8
  122.9 5.0 %collective-permute-start.1 = (f32[5,1,16,128]{3,2,1,0:T(8,128)S(1)}, f32[5,1,16,128]{3,2,1,0:T(8,128)S(1)}, u32[]{:S(2)}, u32[]{:S(2)}) collective-permute-start(f32[5,1,16,128]{3,2,1,0:T(8,128)S(1)} %get-tuple-element.53), channel_id=1, source_target_pairs={{32,0},{64,32},{96,64},{128,96},{160,128},{192,160},{224,192},{0,2... | collective-permute-start | bytes 122888 | tf_op jit(solution)/shard_map/ppermute | solution.py:350
  128.2 5.0 %all-to-all-start.1 = ((f32[32,12,128]{2,1,0:T(8,128)}), f32[32,12,128]{2,1,0:T(8,128)S(1)}, u32[]{:S(2)}, u32[]{:S(2)}) async-start(f32[32,12,128]{2,1,0:T(8,128)} %get-tuple-element.9), calls=%async_computation.1 | async-start | bytes 524288 | tf_op jit(solution)/shard_map/all_to_all | solution.py:364
  133.3 1.1 collective-permute-done
  134.4 1.8 %collective-permute-start.3 = (f32[5,16,1,128]{3,1,2,0:T(8,128)S(1)}, f32[5,16,1,128]{3,1,2,0:T(8,128)S(1)}, u32[]{:S(2)}, u32[]{:S(2)}) collective-permute-start(f32[5,16,1,128]{3,1,2,0:T(8,128)S(1)} %constant_dynamic-update-slice_fusion.15), channel_id=1, source_target_pairs={{4,0},{8,4},{12,8},{16,12},{20,16},{24,20},{28,24},{0,28},{5,1},{9... | collective-permute-start | bytes 122888 | tf_op jit(solution)/shard_map/ppermute | solution.py:350
  138.1 3.8 %collective-permute-done.3 = f32[5,16,1,128]{3,1,2,0:T(8,128)S(1)} collective-permute-done((f32[5,16,1,128]{3,1,2,0:T(8,128)S(1)}, f32[5,16,1,128]{3,1,2,0:T(8,128)S(1)}, u32[]{:S(2)}, u32[]{:S(2)}) %collective-permute-start.3) | collective-permute-done | bytes 40992 | tf_op jit(solution)/shard_map/ppermute | solution.py:350
  142.6 1.3 collective-permute-start.5
  144.5 1.2 collective-permute-start.4
  145.7 0.7 copy_dynamic-update-slice_fusion.6
  149.0 0.8 fusion.33
  149.8 0.8 fusion.34
  150.5 0.7 copy_dynamic-update-slice_fusion.4
  152.6 0.7 copy_dynamic-update-slice_fusion.1
  153.3 0.8 fusion.22
  154.1 0.8 fusion.19
  154.9 0.8 fusion.16
  155.7 0.8 fusion.13
  156.4 0.8 fusion.10
  157.2 0.7 copy_dynamic-update-slice_fusion
  157.9 0.8 fusion.5
  158.7 0.8 fusion.2
  160.2 2.1 %combine.1 = f32[28,3,128]{2,1,0:T(4,128)} custom-call(s32[28,2]{1,0:T(8,128)} %get-tuple-element.8.tgt_ref, f32[32,12,128]{2,1,0:T(8,128)} %copy-done.2), custom_call_target="tpu_custom_call" | custom-call | tf_op jit(solution)/shard_map/combine/pallas_call | solution.py:331
  162.3 1.4 copy.560
  (85 shorter events, 8.3 us)
Async XLA Ops:
  0.6 46.8 %copy-start.1 = (s32[16,16,128]{2,1,0:T(8,128)S(1)}, s32[16,16,128]{2,1,0:T(8,128)}, u32[]{:S(2)}) copy-start(s32[16,16,128]{2,1,0:T(8,128)} %solid_ref.1) | copy-start | bytes 393220
  47.4 1.7 %copy-start = (f32[19,16,16,128]{3,2,1,0:T(8,128)S(1)}, f32[19,16,16,128]{3,2,1,0:T(8,128)}, u32[]{:S(2)}) copy-start(f32[19,16,16,128]{3,2,1,0:T(8,128)} %pop_ref.1) | copy-start | bytes 7471108
  122.9 10.3 %collective-permute-start.1 = (f32[5,1,16,128]{3,2,1,0:T(8,128)S(1)}, f32[5,1,16,128]{3,2,1,0:T(8,128)S(1)}, u32[]{:S(2)}, u32[]{:S(2)}) collective-permute-start(f32[5,1,16,128]{3,2,1,0:T(8,128)S(1)} %get-tuple-element.53), channel_id=1, source_target_pairs={{32,0},{64,32},{96,64},{128,96},{160,128},{192,160},{224,192},{0,2... | collective-permute-start | bytes 122888 | tf_op jit(solution)/shard_map/ppermute | solution.py:350
  127.9 6.5 %collective-permute-start = (f32[5,1,16,128]{3,2,1,0:T(8,128)S(1)}, f32[5,1,16,128]{3,2,1,0:T(8,128)S(1)}, u32[]{:S(2)}, u32[]{:S(2)}) collective-permute-start(f32[5,1,16,128]{3,2,1,0:T(8,128)S(1)} %get-tuple-element.54), channel_id=1, source_target_pairs={{0,32},{32,64},{64,96},{96,128},{128,160},{160,192},{192,224},{224... | collective-permute-start | bytes 122888 | tf_op jit(solution)/shard_map/ppermute | solution.py:349
  128.2 31.2 %all-to-all-start.1 = ((f32[32,12,128]{2,1,0:T(8,128)}), f32[32,12,128]{2,1,0:T(8,128)S(1)}, u32[]{:S(2)}, u32[]{:S(2)}) async-start(f32[32,12,128]{2,1,0:T(8,128)} %get-tuple-element.9), calls=%async_computation.1 | async-start | bytes 524288 | tf_op jit(solution)/shard_map/all_to_all | solution.py:364
  134.4 7.5 %collective-permute-start.3 = (f32[5,16,1,128]{3,1,2,0:T(8,128)S(1)}, f32[5,16,1,128]{3,1,2,0:T(8,128)S(1)}, u32[]{:S(2)}, u32[]{:S(2)}) collective-permute-start(f32[5,16,1,128]{3,1,2,0:T(8,128)S(1)} %constant_dynamic-update-slice_fusion.15), channel_id=1, source_target_pairs={{4,0},{8,4},{12,8},{16,12},{20,16},{24,20},{28,24},{0,28},{5,1},{9... | collective-permute-start | bytes 122888 | tf_op jit(solution)/shard_map/ppermute | solution.py:350
  136.2 6.3 %collective-permute-start.2 = (f32[5,16,1,128]{3,1,2,0:T(8,128)S(1)}, f32[5,16,1,128]{3,1,2,0:T(8,128)S(1)}, u32[]{:S(2)}, u32[]{:S(2)}) collective-permute-start(f32[5,16,1,128]{3,1,2,0:T(8,128)S(1)} %constant_dynamic-update-slice_fusion.10), channel_id=1, source_target_pairs={{0,4},{4,8},{8,12},{12,16},{16,20},{20,24},{24,28},{28,0},{1,5},{5... | collective-permute-start | bytes 122888 | tf_op jit(solution)/shard_map/ppermute | solution.py:349
  142.6 4.5 %collective-permute-start.5 = (f32[5,16,16,1]{2,1,3,0:T(8,128)S(1)}, f32[5,16,16,1]{2,1,3,0:T(8,128)S(1)}, u32[]{:S(2)}, u32[]{:S(2)}) collective-permute-start(f32[5,16,16,1]{2,1,3,0:T(8,128)S(1)} %constant_dynamic-update-slice_fusion.25), channel_id=1, source_target_pairs={{1,0},{2,1},{3,2},{0,3},{5,4},{6,5},{7,6},{4,7},{9,8},{10,9},{11,1... | collective-permute-start | bytes 15368 | tf_op jit(solution)/shard_map/ppermute | solution.py:350
  144.5 3.2 %collective-permute-start.4 = (f32[5,16,16,1]{2,1,3,0:T(8,128)S(1)}, f32[5,16,16,1]{2,1,3,0:T(8,128)S(1)}, u32[]{:S(2)}, u32[]{:S(2)}) collective-permute-start(f32[5,16,16,1]{2,1,3,0:T(8,128)S(1)} %constant_dynamic-update-slice_fusion.20), channel_id=1, source_target_pairs={{0,1},{1,2},{2,3},{3,0},{4,5},{5,6},{6,7},{7,4},{8,9},{9,10},{10,1... | collective-permute-start | bytes 15368 | tf_op jit(solution)/shard_map/ppermute | solution.py:349
  159.5 0.7 copy-start.2

commit v2 on v1

--- a/solution.py
+++ b/solution.py
@@ -43,40 +43,40 @@
 OUTSIDE = -100.0
 
 
-def prep_kernel(inter_ref, pos_ref, anc_ref, cell_ref, w_ref, out_ref, tgt_ref, count_ref):
-    root_x = lax.axis_index("gx") * 16
-
-    def clear_count(b, carry):
+def prep_kernel(inter_ref, pos_ref, anc_ref, cell_ref, w_ref, out_ref, tgt_ref, count_ref, force_ref):
+    my_x, my_y, my_z = lax.axis_index("gx"), lax.axis_index("gy"), lax.axis_index("gz")
+
+    def clear(b, carry):
         count_ref[b] = 0
-        return carry
-
-    lax.fori_loop(0, BRICKS, clear_count, 0)
-
-    def clear(b, carry):
         out_ref[b, 0:44] = jnp.zeros((44, VERT), F32)
         out_ref[b, 44:56] = jnp.full((12, VERT), OUTSIDE, F32)
         return carry
 
     lax.fori_loop(0, BRICKS, clear, 0)
+    for c in range(3):
+        pos = pos_ref[c]
+        cycle = pltpu.roll(pos, 1, 1) + pltpu.roll(pos, VERT - 1, 1) - 2.0 * pos
+        force_ref[c] = TENSION * cycle + TETHER * (anc_ref[c] - pos)
 
     def patch(p, carry):
-        pos = pos_ref[p]
-        cycle = pltpu.roll(pos, 1, 1) + pltpu.roll(pos, VERT - 1, 1) - 2.0 * pos
-        force = TENSION * cycle + TETHER * (anc_ref[p] - pos)
-        cell = cell_ref[p]
+        one = pl.ds(p, 1)
         weight = w_ref[p]
+        force = [force_ref[c, one] for c in range(3)]
+        x, y, z = cell_ref[0, one] - my_x * 16, cell_ref[1, one], cell_ref[2, one]
         for j in range(2):
-            b = inter_ref[p, j]
+            b = inter_ref[j, p]
             r = count_ref[b]
             count_ref[b] = r + 1
-            tgt_ref[p, j] = b * SLOT_CAP + r
-            x = cell[0:1] - root_x
-            y = cell[1:2] - (b // 4) * 16
-            z = cell[2:3] - (b % 4) * 128
-            inside = (x >= 0) & (x < 16) & (y >= 0) & (y < 16) & (z >= 0) & (z < 128)
+            by, bz = b // 4, b % 4
+            away = (by - my_y + 8) % 8
+            turn = jnp.where(away == 0, 0, jnp.where(away <= 4, 2 * away - 1, 2 * (8 - away)))
+            tgt_ref[j, p] = (turn * 4 + (bz - my_z + 4) % 4) * SLOT_CAP + r
+            local_y, local_z = y - by * 16, z - bz * 128
+            inside = (x >= 0) & (x < 16) & (local_y >= 0) & (local_y < 16)
+            inside = inside & (local_z >= 0) & (local_z < 128)
             out_ref[b, pl.ds(pl.multiple_of(r * 8, 8), 8)] = weight
-            for a, coord in enumerate((x, y, z)):
-                out_ref[b, pl.ds(32 + 4 * a + r, 1)] = force[a : a + 1]
+            for a, coord in enumerate((x, local_y, local_z)):
+                out_ref[b, pl.ds(32 + 4 * a + r, 1)] = force[a]
                 out_ref[b, pl.ds(44 + 4 * a + r, 1)] = jnp.where(
                     inside, coord.astype(F32), OUTSIDE
                 )
@@ -93,11 +93,14 @@
         name="prep",
         out_shape=(
             jax.ShapeDtypeStruct((BRICKS, ROWS, VERT), F32),
-            jax.ShapeDtypeStruct((PATCH_DEV, 2), jnp.int32),
+            jax.ShapeDtypeStruct((2, PATCH_DEV), jnp.int32),
         ),
         in_specs=[smem, vmem, vmem, vmem, vmem],
         out_specs=(vmem, smem),
-        scratch_shapes=[pltpu.SMEM((BRICKS,), jnp.int32)],
+        scratch_shapes=[
+            pltpu.SMEM((BRICKS,), jnp.int32),
+            pltpu.VMEM((3, PATCH_DEV, VERT), F32),
+        ],
     )(intersection, positions, anchors, base_cell, weights)
 
 
@@ -106,7 +109,7 @@
     return high, (value - high.astype(F32)).astype(BF16)
 
 
-def scatter_chunk(tab_ref, i, a_ref, z_ref, acc_ref):
+def scatter_factors(tab_ref, i, base_col, a_ref, z_ref):
     y_iota = lax.broadcasted_iota(jnp.int32, (16, VERT), 0).astype(F32)
     z_iota = lax.broadcasted_iota(jnp.int32, (256, VERT), 0).astype(F32)
     zero16 = jnp.zeros((16, VERT), BF16)
@@ -117,8 +120,9 @@
         upper = x >= 8.0
         x_in = jnp.where(upper, x - 8.0, x)
         column = jnp.where(upper, z + 128.0, z)
-        lanes = slice(s * VERT, (s + 1) * VERT)
-        z_ref[:, lanes] = jnp.where(z_iota == column, 1.0, 0.0).astype(BF16)
+        hot = jnp.where(z_iota == column, 1.0, 0.0).astype(BF16)
+        for hl in range(2):
+            z_ref[:, pl.ds(base_col + hl * 512 + s * VERT, VERT)] = hot
         at_y = y_iota == y
         at_y1 = y_iota - 1.0 == y
         x_wide = jnp.broadcast_to(x_in, (16, VERT)).astype(BF16)
@@ -133,20 +137,13 @@
                     parts.append(halves(jnp.where(at_y, w0, jnp.where(at_y1, w1, 0.0))))
                 base = (kz * 3 + c) * HALF
                 for hl in range(2):
-                    col = slice(hl * 512 + s * VERT, hl * 512 + (s + 1) * VERT)
+                    col = pl.ds(base_col + hl * 512 + s * VERT, VERT)
                     for plane in range(9):
                         a_ref[base + plane * 16 : base + plane * 16 + 16, col] = jnp.where(
                             masks[plane + 1],
                             parts[0][hl],
                             jnp.where(masks[plane], parts[1][hl], zero16),
                         )
-    zz = z_ref[...]
-    for block in range(6):
-        rows = slice(block * HALF, (block + 1) * HALF)
-        dims = (((1,), (1,)), ((), ()))
-        acc_ref[rows] += lax.dot_general(
-            a_ref[rows, 0:512], zz, dims, preferred_element_type=F32
-        ) + lax.dot_general(a_ref[rows, 512:1024], zz, dims, preferred_element_type=F32)
 
 
 def finish_force(acc_ref, force_ref):
@@ -268,102 +265,309 @@
             ret_ref[i, pl.ds(4 * c + s, 1)] = jnp.sum(both, axis=0, keepdims=True)
 
 
-def core_kernel(
-    tab_ref, pop_ref, solid_ref, post_ref, ret_ref, a_ref, z_ref, acc_ref, force_ref, vel_ref, vt_ref, b_ref
+PLUS = [[q for q in range(19) if VELOCITIES[q][a] == 1] for a in range(3)]
+MINUS = [[q for q in range(19) if VELOCITIES[q][a] == -1] for a in range(3)]
+MESH = pl.DeviceIdType.MESH
+
+
+def offset_of(i):
+    j, dz = i // 4, i % 4
+    half = (j + 1) // 2
+    odd = j % 2
+    return odd * half + (1 - odd) * ((8 - half) % 8), dz
+
+
+def shift_x(post_ref, halo_ref):
+    for k, q in enumerate(PLUS[0]):
+        moved = post_ref[q, 0:15]
+        post_ref[q, 1:16] = moved
+        post_ref[q, 0] = halo_ref[0, k]
+    for k, q in enumerate(MINUS[0]):
+        moved = post_ref[q, 1:16]
+        post_ref[q, 0:15] = moved
+        post_ref[q, 15] = halo_ref[1, k]
+
+
+def shift_y(post_ref, halo_ref):
+    row = lax.broadcasted_iota(jnp.int32, (256, 128), 0) % 16
+    for side, (directions, by, edge) in enumerate(((PLUS[1], 1, 0), (MINUS[1], 255, 15))):
+        for k, q in enumerate(directions):
+            moved = pltpu.roll(post_ref[q].reshape(256, 128), by, 0)
+            halo = jnp.broadcast_to(halo_ref[side, k][:, None, :], (16, 16, 128)).reshape(256, 128)
+            post_ref[q] = jnp.where(row == edge, halo, moved).reshape(16, 16, 128)
+
+
+def turn_z(post_ref, send_ref):
+    lane = lax.broadcasted_iota(jnp.int32, (256, 128), 1)
+    for side, (directions, by, to) in enumerate(((PLUS[2], 1, 0), (MINUS[2], 127, 1))):
+        packed = jnp.zeros((256, 128), F32)
+        for k, q in enumerate(directions):
+            moved = pltpu.roll(post_ref[q].reshape(256, 128), by, 1)
+            post_ref[q] = moved.reshape(16, 16, 128)
+            packed = jnp.where(lane == k, pltpu.roll(moved, k + to, 1) if k + to else moved, packed)
+        send_ref[side] = packed
+
+
+def shift_z(post_ref, halo_ref):
+    lane = lax.broadcasted_iota(jnp.int32, (256, 128), 1)
+    for side, (directions, edge) in enumerate(((PLUS[2], 0), (MINUS[2], 127))):
+        packed = halo_ref[side]
+        for k, q in enumerate(directions):
+            by = (edge - k) % 128
+            halo = pltpu.roll(packed, by, 1) if by else packed
+            old = post_ref[q].reshape(256, 128)
+            post_ref[q] = jnp.where(lane == edge, halo, old).reshape(16, 16, 128)
+
+
+def step_kernel(
+    out_ref, tgt_ref, pop_hbm, solid_hbm, read_hbm, vertex_ref,
+    tab_ref, pop_ref, solid_ref, post_ref, a_ref, z_ref, acc_ref, force_ref, vel_ref, vt_ref, b_ref,
+    ret_ref, back_ref, xs_ref, xr_ref, ys_ref, yr_ref, zs_ref, zr_ref,
+    tab_send, tab_recv, ret_send, ret_recv, halo_send, halo_recv, load_sem, store_sem,
 ):
+    my_x, my_y, my_z = lax.axis_index("gx"), lax.axis_index("gy"), lax.axis_index("gz")
+    load_pop = pltpu.make_async_copy(pop_hbm, pop_ref, load_sem.at[0])
+    load_solid = pltpu.make_async_copy(solid_hbm, solid_ref, load_sem.at[1])
+    load_pop.start()
+    load_solid.start()
+
+    def ahead(i):
+        dy, dz = offset_of(i)
+        return (my_x, lax.rem(my_y + dy, 8), lax.rem(my_z + dz, 4))
+
+    def behind(i):
+        dy, dz = offset_of(i)
+        return (my_x, lax.rem(my_y + 8 - dy, 8), lax.rem(my_z + 4 - dz, 4))
+
+    up_x = (lax.rem(my_x + 1, 8), my_y, my_z)
+    down_x = (lax.rem(my_x + 7, 8), my_y, my_z)
+    up_y = (my_x, lax.rem(my_y + 1, 8), my_z)
+    down_y = (my_x, lax.rem(my_y + 7, 8), my_z)
+    up_z = (my_x, my_y, lax.rem(my_z + 1, 4))
+    down_z = (my_x, my_y, lax.rem(my_z + 3, 4))
+
+    barrier = pltpu.get_barrier_semaphore()
+
+    def greet(i, carry):
+        pl.semaphore_signal(barrier, inc=1, device_id=ahead(i), device_id_type=MESH)
+        return carry
+
+    lax.fori_loop(1, BRICKS, greet, 0)
+    pl.semaphore_signal(barrier, inc=1, device_id=up_x, device_id_type=MESH)
+    pl.semaphore_signal(barrier, inc=1, device_id=down_x, device_id_type=MESH)
+    pl.semaphore_wait(barrier, BRICKS + 1)
+
+    def table_copy(i):
+        to = ahead(i)
+        return pltpu.make_async_remote_copy(
+            src_ref=out_ref.at[to[1] * 4 + to[2]],
+            dst_ref=tab_ref.at[i],
+            send_sem=tab_send.at[i],
+            recv_sem=tab_recv.at[i],
+            device_id=to,
+            device_id_type=MESH,
+        )
+
+    def return_copy(i):
+        return pltpu.make_async_remote_copy(
+            src_ref=ret_ref.at[i],
+            dst_ref=back_ref.at[i],
+            send_sem=ret_send.at[i],
+            recv_sem=ret_recv.at[i],
+            device_id=behind(i),
+            device_id_type=MESH,
+        )
+
+    def send_table(i, carry):
+        table_copy(i).start()
+        return carry
+
+    lax.fori_loop(1, BRICKS, send_table, 0)
+    tab_ref[0] = out_ref[my_y * 4 + my_z]
     acc_ref[...] = jnp.zeros_like(acc_ref)
 
-    def scatter(i, carry):
-        scatter_chunk(tab_ref, i, a_ref, z_ref, acc_ref)
-        return carry
-
-    lax.fori_loop(0, BRICKS, scatter, 0)
+    def scatter(t, carry):
+        @pl.when(t > 0)
+        def _():
+            table_copy(2 * t).wait_recv()
+
+        table_copy(2 * t + 1).wait_recv()
+        for j in range(2):
+            scatter_factors(tab_ref, 2 * t + j, j * 1024, a_ref, z_ref)
+        acc_ref[...] += lax.dot_general(
+            a_ref[...], z_ref[...], (((1,), (1,)), ((), ())), preferred_element_type=F32
+        )
+        return carry
+
+    lax.fori_loop(0, BRICKS // 2, scatter, 0)
     finish_force(acc_ref, force_ref)
+    load_pop.wait()
+    load_solid.wait()
     collide_all(pop_ref, solid_ref, force_ref, post_ref, vel_ref)
+
+    def halo_copy(k, src, dst, to):
+        return pltpu.make_async_remote_copy(
+            src_ref=src,
+            dst_ref=dst,
+            send_sem=halo_send.at[k],
+            recv_sem=halo_recv.at[k],
+            device_id=to,
+            device_id_type=MESH,
+        )
+
+    halo = [
+        halo_copy(0, xs_ref.at[0], xr_ref.at[0], up_x),
+        halo_copy(1, xs_ref.at[1], xr_ref.at[1], down_x),
+        halo_copy(2, ys_ref.at[0], yr_ref.at[0], up_y),
+        halo_copy(3, ys_ref.at[1], yr_ref.at[1], down_y),
+        halo_copy(4, zs_ref.at[0], zr_ref.at[0], up_z),
+        halo_copy(5, zs_ref.at[1], zr_ref.at[1], down_z),
+    ]
+    for k in range(5):
+        xs_ref[0, k] = post_ref[PLUS[0][k], 15]
+        xs_ref[1, k] = post_ref[MINUS[0][k], 0]
+    halo[0].start()
+    halo[1].start()
     transpose_velocity(vel_ref, vt_ref)
 
-    def gather(i, carry):
-        gather_chunk(tab_ref, i, b_ref, vt_ref, ret_ref)
-        return carry
-
-    lax.fori_loop(0, BRICKS, gather, 0)
-
-
-def core(table, populations, solid_flags):
+    def store_copy(q):
+        return pltpu.make_async_copy(post_ref.at[q], read_hbm.at[q], store_sem.at[q])
+
+    along_z = PLUS[2] + MINUS[2]
+
+    def gather(t, carry):
+        for j in range(2):
+            i = BRICKS - 1 - (2 * t + j)
+            gather_chunk(tab_ref, i, b_ref, vt_ref, ret_ref)
+
+            @pl.when(i > 0)
+            def _():
+                return_copy(i).start()
+
+        @pl.when(t == 3)
+        def _():
+            halo[0].wait_recv()
+            halo[1].wait_recv()
+            shift_x(post_ref, xr_ref)
+            for k in range(5):
+                ys_ref[0, k] = post_ref[PLUS[1][k], :, 15, :]
+                ys_ref[1, k] = post_ref[MINUS[1][k], :, 0, :]
+            halo[2].start()
+            halo[3].start()
+
+        @pl.when(t == 7)
+        def _():
+            halo[2].wait_recv()
+            halo[3].wait_recv()
+            shift_y(post_ref, yr_ref)
+            for q in range(19):
+                if q not in along_z:
+                    store_copy(q).start()
+            turn_z(post_ref, zs_ref)
+            halo[4].start()
+            halo[5].start()
+
+        @pl.when(t == 11)
+        def _():
+            halo[4].wait_recv()
+            halo[5].wait_recv()
+            shift_z(post_ref, zr_ref)
+            for q in along_z:
+                store_copy(q).start()
+
+        return carry
+
+    lax.fori_loop(0, BRICKS // 2, gather, 0)
+    back_ref[0] = ret_ref[0]
+
+    def wait_return(i, carry):
+        return_copy(i).wait_recv()
+        return carry
+
+    lax.fori_loop(1, BRICKS, wait_return, 0)
+
+    def patch(p, carry):
+        first, second = tgt_ref[0, p], tgt_ref[1, p]
+        for c in range(3):
+            vertex_ref[c, pl.ds(p, 1)] = (
+                back_ref[first // SLOT_CAP, pl.ds(4 * c + first % SLOT_CAP, 1)]
+                + back_ref[second // SLOT_CAP, pl.ds(4 * c + second % SLOT_CAP, 1)]
+            )
+        return carry
+
+    lax.fori_loop(0, PATCH_DEV, patch, 0)
+
+    def wait_sends(i, carry):
+        table_copy(i).wait_send()
+        return_copy(i).wait_send()
+        return carry
+
+    lax.fori_loop(1, BRICKS, wait_sends, 0)
+    for copy in halo:
+        copy.wait_send()
+    for q in range(19):
+        store_copy(q).wait()
+
+
+def step(outgoing, target, populations, solid_flags):
     vmem = pl.BlockSpec(memory_space=pltpu.VMEM)
+    smem = pl.BlockSpec(memory_space=pltpu.SMEM)
+    anywhere = pl.BlockSpec(memory_space=pl.ANY)
+    dma = pltpu.SemaphoreType.DMA
     return pl.pallas_call(
-        core_kernel,
-        name="core",
+        step_kernel,
+        name="step",
         out_shape=(
             jax.ShapeDtypeStruct(populations.shape, F32),
-            jax.ShapeDtypeStruct((BRICKS, 12, VERT), F32),
+            jax.ShapeDtypeStruct((3, PATCH_DEV, VERT), F32),
         ),
-        in_specs=[vmem] * 3,
-        out_specs=(vmem, vmem),
+        in_specs=[vmem, smem, anywhere, anywhere],
+        out_specs=(anywhere, vmem),
         scratch_shapes=[
-            pltpu.VMEM((6 * HALF, 1024), BF16),
-            pltpu.VMEM((256, 512), BF16),
+            pltpu.VMEM((BRICKS, ROWS, VERT), F32),
+            pltpu.VMEM((19, 16, 16, 128), F32),
+            pltpu.VMEM((16, 16, 128), jnp.int32),
+            pltpu.VMEM((19, 16, 16, 128), F32),
+            pltpu.VMEM((6 * HALF, 2048), BF16),
+            pltpu.VMEM((256, 2048), BF16),
             pltpu.VMEM((6 * HALF, 256), F32),
             pltpu.VMEM((3, 256, 128), F32),
             pltpu.VMEM((3, 256, 128), F32),
             pltpu.VMEM((384, 768), BF16),
             pltpu.VMEM((4, 768, 256), BF16),
+            pltpu.VMEM((BRICKS, 12, VERT), F32),
+            pltpu.VMEM((BRICKS, 12, VERT), F32),
+            pltpu.VMEM((2, 5, 16, 128), F32),
+            pltpu.VMEM((2, 5, 16, 128), F32),
+            pltpu.VMEM((2, 5, 16, 128), F32),
+            pltpu.VMEM((2, 5, 16, 128), F32),
+            pltpu.VMEM((2, 256, 128), F32),
+            pltpu.VMEM((2, 256, 128), F32),
+            dma((BRICKS,)),
+            dma((BRICKS,)),
+            dma((BRICKS,)),
+            dma((BRICKS,)),
+            dma((6,)),
+            dma((6,)),
+            dma((2,)),
+            dma((19,)),
         ],
-        compiler_params=pltpu.CompilerParams(vmem_limit_bytes=32 * 1024 * 1024),
-    )(table, populations, solid_flags)
-
-
-def combine_kernel(tgt_ref, returned_ref, out_ref):
-    def patch(p, carry):
-        first, second = tgt_ref[p, 0], tgt_ref[p, 1]
-        for c in range(3):
-            out_ref[p, c : c + 1] = (
-                returned_ref[first // SLOT_CAP, pl.ds(4 * c + first % SLOT_CAP, 1)]
-                + returned_ref[second // SLOT_CAP, pl.ds(4 * c + second % SLOT_CAP, 1)]
-            )
-        return carry
-
-    lax.fori_loop(0, PATCH_DEV, patch, 0)
-
-
-def combine(target, returned):
-    vmem = pl.BlockSpec(memory_space=pltpu.VMEM)
-    return pl.pallas_call(
-        combine_kernel,
-        name="combine",
-        out_shape=jax.ShapeDtypeStruct((PATCH_DEV, 3, VERT), F32),
-        in_specs=[pl.BlockSpec(memory_space=pltpu.SMEM), vmem],
-        out_specs=vmem,
-    )(target, returned)
-
-
-def stream(post):
-    lists = [post[q] for q in range(19)]
-    for dim, axis in enumerate(("gx", "gy", "gz")):
-        plus = [q for q in range(19) if VELOCITIES[q][dim] == 1]
-        minus = [q for q in range(19) if VELOCITIES[q][dim] == -1]
-        size = lists[0].shape[dim]
-        count = lax.axis_size(axis)
-        up = jnp.stack([lax.slice_in_dim(lists[q], size - 1, size, axis=dim) for q in plus])
-        down = jnp.stack([lax.slice_in_dim(lists[q], 0, 1, axis=dim) for q in minus])
-        before = lax.ppermute(up, axis, [(i, (i + 1) % count) for i in range(count)])
-        after = lax.ppermute(down, axis, [((i + 1) % count, i) for i in range(count)])
-        for k, q in enumerate(plus):
-            body = lax.slice_in_dim(lists[q], 0, size - 1, axis=dim)
-            lists[q] = jnp.concatenate([before[k], body], axis=dim)
-        for k, q in enumerate(minus):
-            body = lax.slice_in_dim(lists[q], 1, size, axis=dim)
-            lists[q] = jnp.concatenate([body, after[k]], axis=dim)
-    return jnp.stack(lists)
+        compiler_params=pltpu.CompilerParams(
+            collective_id=0, has_side_effects=True, vmem_limit_bytes=40 * 1024 * 1024
+        ),
+    )(outgoing, target, populations, solid_flags)
 
 
 def body(populations, solid_flags, positions, anchors, base_cell, weights, intersection):
-    outgoing, target = prep(intersection, positions, anchors, base_cell, weights)
-    table = lax.all_to_all(outgoing, ("gy", "gz"), split_axis=0, concat_axis=0, tiled=True)
-    post, summed = core(table, populations, solid_flags)
-    returned = lax.all_to_all(summed, ("gy", "gz"), split_axis=0, concat_axis=0, tiled=True)
-    vertex_velocity = combine(target, returned)
-    return (stream(post), vertex_velocity)
+    outgoing, target = prep(
+        intersection.T,
+        jnp.transpose(positions, (1, 0, 2)),
+        jnp.transpose(anchors, (1, 0, 2)),
+        jnp.transpose(base_cell, (1, 0, 2)),
+        weights,
+    )
+    read, vertex = step(outgoing, target, populations, solid_flags)
+    return (read, jnp.transpose(vertex, (1, 0, 2)))
 
 
 def solution(mesh):

time: 164 us -> 93.1 us (0.57)
  blocking collectives: 36.4 us -> 0 us
  starting transfers between devices: 14.3 us -> 0 us
  local copies, waits for them, and re-layouts: 18.6 us -> 6.53 us
  other arithmetic: 9.6 us -> 0 us
  Pallas kernels: 78.5 us -> 85.7 us
  waiting for transfers between devices: 5.28 us -> 0 us
    all_to_all x1 -> x0, blocking collectives: 36.4 us -> none  [body(): lax.all_to_all(outgoing, ('gy', 'gz'), split_axis=0, concat_axis=0, tiled...]
    ppermute x6 -> x0, starting transfers between devices: 9.27 us -> none  [the longest x3 8.08 us: stream(): lax.ppermute(down, axis, [((i + 1) % count, i) for i in range(count)])]
    pallas_call x2 -> x1, Pallas kernels: 73.9 us -> 82.2 us  [step(): pl.pallas_call(step_kernel, name='step', out_shape=(jax.ShapeDtypeStruct(...]
    unnamed x34 -> x10, local copies, waits for them, and re-layouts: 14.5 us -> 6.53 us
    unnamed x13 -> x0, other arithmetic: 7.57 us -> none
    ppermute x6 -> x0, waiting for transfers between devices: 5.28 us -> none  [the longest x3 3.85 us: stream(): lax.ppermute(down, axis, [((i + 1) % count, i) for i in range(count)])]
    all_to_all x1 -> x0, starting transfers between devices: 4.98 us -> none  [body(): lax.all_to_all(summed, ('gy', 'gz'), split_axis=0, concat_axis=0, tiled=T...]
    squeeze x18 -> x0, local copies, waits for them, and re-layouts: 2.48 us -> none  [the longest x8 0.87 us: stream(): lists[q] = jnp.concatenate([body, after[k]], axis=dim)]
  transfers between devices with their start and end apart: 7 -> 0, of which waited for: 3 -> 0; matrix products, arithmetic and copies ran while one was open for 10% -> 0% of each run, Pallas kernels for 0% -> 0%
where the time goes in v2:
time: 93.1 us; the launch traced here: 92.9 us
  Pallas kernels  85.7 us (92%)
  local copies, waits for them, and re-layouts  6.53 us (7%)
    pallas_call x1, Pallas kernels, step(): pl.pallas_call(step_kernel, name='step', out_shape=(jax.ShapeDtypeStruct(...  82.2 us
    unnamed x10, local copies, waits for them, and re-layouts  6.53 us
    pallas_call x1, Pallas kernels, prep(): pl.pallas_call(prep_kernel, name='prep', out_shape=(jax.ShapeDtypeStruct(...  3.46 us

profile of v2, /device:TPU:1, one launch (start us, length us, event | category | flops | bytes accessed | tf_op | source)
XLA Modules:
  0.0 92.9 jit_solution(17110308659699803536)
XLA Ops:
  0.6 3.5 %prep.1 = (f32[32,56,128]{2,1,0:T(8,128)}, s32[2,28]{1,0:T(2,128)}) custom-call(s32[2,28]{1,0:T(2,128)} %bitcast.9, f32[3,28,128]{2,1,0:T(8,128)} %bitcast.6, f32[3,28,128]{2,1,0:T(8,128)} %bitcast.7, s32[3,28,128]{2,1,0:T(8,128)} %bitcast.8, f32[28,8,128]{2,1,0:T(8,128)} %w_ref.1), custom_call_target="tpu_custom_call" | custom-call | tf_op jit(solution)/shard_map/prep/pallas_call | solution.py:91
  4.1 0.0 copy-start
  4.1 1.7 %copy-done = f32[19,16,16,128]{3,2,1,0:T(8,128)S(1)} copy-done((f32[19,16,16,128]{3,2,1,0:T(8,128)S(1)}, f32[19,16,16,128]{3,2,1,0:T(8,128)}, u32[]{:S(2)}) %copy-start) | copy-done | bytes 2490392
  5.8 0.0 copy-start.1
  5.8 1.2 %copy-done.1 = f32[32,56,128]{2,1,0:T(8,128)S(1)} copy-done((f32[32,56,128]{2,1,0:T(8,128)S(1)}, f32[32,56,128]{2,1,0:T(8,128)}, u32[]{:S(2)}) %copy-start.1) | copy-done | bytes 917528
  7.0 0.0 copy-start.2
  7.0 0.9 copy-done.2
  7.9 0.0 copy-start.3
  7.9 0.7 copy-done.3
  8.6 82.2 %step.1 = (f32[19,16,16,128]{3,2,1,0:T(8,128)S(1)}, f32[3,28,128]{2,1,0:T(8,128)S(1)}) custom-call(f32[32,56,128]{2,1,0:T(8,128)S(1)} %copy-done.1, s32[2,28]{1,0:T(2,128)S(1)} %copy-done.3, f32[19,16,16,128]{3,2,1,0:T(8,128)S(1)} %copy-done, s32[16,16,128]{2,1,0:T(8,128)S(1)} %copy-done.2), custom_call_target="tpu_custom_call" | custom-call | tf_op jit(solution)/shard_map/step/pallas_call | solution.py:517
  90.8 1.5 %copy.11 = f32[19,16,16,128]{3,2,1,0:T(8,128)} copy(f32[19,16,16,128]{3,2,1,0:T(8,128)S(1)} %get-tuple-element.12) | data formatting | bytes 4980736
  92.3 0.6 copy.12
Async XLA Ops:
  4.1 1.7 %copy-start = (f32[19,16,16,128]{3,2,1,0:T(8,128)S(1)}, f32[19,16,16,128]{3,2,1,0:T(8,128)}, u32[]{:S(2)}) copy-start(f32[19,16,16,128]{3,2,1,0:T(8,128)} %pop_hbm.1) | copy-start | bytes 7471108
  5.8 1.2 %copy-start.1 = (f32[32,56,128]{2,1,0:T(8,128)S(1)}, f32[32,56,128]{2,1,0:T(8,128)}, u32[]{:S(2)}) copy-start(f32[32,56,128]{2,1,0:T(8,128)} %get-tuple-element.6.out_ref) | copy-start | bytes 2752516
  7.0 0.9 copy-start.2
  7.9 0.7 copy-start.3

commit v3 on v2

--- a/solution.py
+++ b/solution.py
@@ -36,77 +36,85 @@
     (0, 1, -1),
     (0, -1, 1),
 ]
-OPPOSITE = [0, 2, 1, 4, 3, 6, 5, 8, 7, 10, 9, 12, 11, 14, 13, 16, 15, 18, 17]
 LATTICE_WEIGHTS = [1.0 / 3.0] + [1.0 / 18.0] * 6 + [1.0 / 36.0] * 12
 F32 = jnp.float32
 BF16 = jnp.bfloat16
 OUTSIDE = -100.0
 
 
-def prep_kernel(inter_ref, pos_ref, anc_ref, cell_ref, w_ref, out_ref, tgt_ref, count_ref, force_ref):
-    my_x, my_y, my_z = lax.axis_index("gx"), lax.axis_index("gy"), lax.axis_index("gz")
-
-    def clear(b, carry):
-        count_ref[b] = 0
-        out_ref[b, 0:44] = jnp.zeros((44, VERT), F32)
-        out_ref[b, 44:56] = jnp.full((12, VERT), OUTSIDE, F32)
-        return carry
-
-    lax.fori_loop(0, BRICKS, clear, 0)
+def halves(value):
+    high = value.astype(BF16)
+    return high, (value - high.astype(F32)).astype(BF16)
+
+
+def thirds(value):
+    high = value.astype(BF16)
+    rest = value - high.astype(F32)
+    middle = rest.astype(BF16)
+    return high, middle, (rest - middle.astype(F32)).astype(BF16)
+
+
+def choose_slots(inter_ref, pad_ref, tgt_ref, my_y, my_z):
+    pad_ref[...] = jnp.full((8, 128), -1, jnp.int32)
+    tgt_ref[...] = jnp.zeros((8, 128), jnp.int32)
+    pad_ref[0:2, 0:PATCH_DEV] = inter_ref[...]
+    lane = lax.broadcasted_iota(jnp.int32, (BRICKS, 128), 1)
+    brick_iota = lax.broadcasted_iota(jnp.int32, (BRICKS, 128), 0)
+    rows = [pad_ref[j : j + 1] for j in range(2)]
+    listed = [(brick_iota == row).astype(jnp.int32) for row in rows]
+    total = listed[0] + listed[1]
+    count = total
+    for by in (1, 2, 4, 8, 16):
+        count = count + jnp.where(lane >= by, pltpu.roll(count, by, 1), 0)
+    before = count - total
+    slots = []
+    for j in range(2):
+        rank = jnp.sum(listed[j] * before, axis=0, keepdims=True)
+        slots.append(rows[j] * SLOT_CAP + rank)
+        away = ((rows[j] >> 2) - my_y + 8) & 7
+        turn = jnp.where(away == 0, 0, jnp.where(away <= 4, 2 * away - 1, 16 - 2 * away))
+        side = ((rows[j] & 3) - my_z + 4) & 3
+        tgt_ref[j : j + 1] = (turn * 4 + side) * SLOT_CAP + rank
+    return slots
+
+
+def make_tables(slots, pos_ref, anc_ref, cell_ref, w_ref, field_ref, part_ref, out_ref, my_x):
+    field_ref[...] = jnp.zeros_like(field_ref)
+    for k in range(8):
+        field_ref[k, 0:PATCH_DEV] = w_ref[:, k, :]
     for c in range(3):
         pos = pos_ref[c]
         cycle = pltpu.roll(pos, 1, 1) + pltpu.roll(pos, VERT - 1, 1) - 2.0 * pos
-        force_ref[c] = TENSION * cycle + TETHER * (anc_ref[c] - pos)
-
-    def patch(p, carry):
-        one = pl.ds(p, 1)
-        weight = w_ref[p]
-        force = [force_ref[c, one] for c in range(3)]
-        x, y, z = cell_ref[0, one] - my_x * 16, cell_ref[1, one], cell_ref[2, one]
-        for j in range(2):
-            b = inter_ref[j, p]
-            r = count_ref[b]
-            count_ref[b] = r + 1
-            by, bz = b // 4, b % 4
-            away = (by - my_y + 8) % 8
-            turn = jnp.where(away == 0, 0, jnp.where(away <= 4, 2 * away - 1, 2 * (8 - away)))
-            tgt_ref[j, p] = (turn * 4 + (bz - my_z + 4) % 4) * SLOT_CAP + r
-            local_y, local_z = y - by * 16, z - bz * 128
-            inside = (x >= 0) & (x < 16) & (local_y >= 0) & (local_y < 16)
-            inside = inside & (local_z >= 0) & (local_z < 128)
-            out_ref[b, pl.ds(pl.multiple_of(r * 8, 8), 8)] = weight
-            for a, coord in enumerate((x, local_y, local_z)):
-                out_ref[b, pl.ds(32 + 4 * a + r, 1)] = force[a]
-                out_ref[b, pl.ds(44 + 4 * a + r, 1)] = jnp.where(
-                    inside, coord.astype(F32), OUTSIDE
-                )
-        return carry
-
-    lax.fori_loop(0, PATCH_DEV, patch, 0)
-
-
-def prep(intersection, positions, anchors, base_cell, weights):
-    vmem = pl.BlockSpec(memory_space=pltpu.VMEM)
-    smem = pl.BlockSpec(memory_space=pltpu.SMEM)
-    return pl.pallas_call(
-        prep_kernel,
-        name="prep",
-        out_shape=(
-            jax.ShapeDtypeStruct((BRICKS, ROWS, VERT), F32),
-            jax.ShapeDtypeStruct((2, PATCH_DEV), jnp.int32),
-        ),
-        in_specs=[smem, vmem, vmem, vmem, vmem],
-        out_specs=(vmem, smem),
-        scratch_shapes=[
-            pltpu.SMEM((BRICKS,), jnp.int32),
-            pltpu.VMEM((3, PATCH_DEV, VERT), F32),
-        ],
-    )(intersection, positions, anchors, base_cell, weights)
-
-
-def halves(value):
-    high = value.astype(BF16)
-    return high, (value - high.astype(F32)).astype(BF16)
+        field_ref[8 + c, 0:PATCH_DEV] = TENSION * cycle + TETHER * (anc_ref[c] - pos)
+        field_ref[11 + c, 0:PATCH_DEV] = cell_ref[c].astype(F32) + 1.0
+    for f in range(14):
+        for k, part in enumerate(thirds(field_ref[f])):
+            part_ref[32 * k : 32 * k + 32, f * VERT : f * VERT + VERT] = part
+    slot_iota = lax.broadcasted_iota(jnp.int32, (128, 128), 0)
+    routed = (slot_iota == slots[0]) | (slot_iota == slots[1])
+    routed = jnp.where(routed, 1.0, 0.0).astype(BF16)[:, 0:32]
+    routed = jnp.concatenate([routed, routed, routed], axis=1)
+    fields = [
+        jnp.dot(routed, part_ref[:, f * VERT : f * VERT + VERT], preferred_element_type=F32)
+        for f in range(14)
+    ]
+    brick = slot_iota // SLOT_CAP
+    roots = (my_x * 16, (brick // 4) * 16, (brick % 4) * 128)
+    cells = [fields[11 + a] - (1 + roots[a]).astype(F32) for a in range(3)]
+    inside = None
+    for cell, size in zip(cells, (16.0, 16.0, 128.0)):
+        within = (cell >= 0.0) & (cell < size)
+        inside = within if inside is None else inside & within
+    for a in range(3):
+        fields[11 + a] = jnp.where(inside, cells[a], OUTSIDE)
+    low = slot_iota % 8 < 4
+    for g in range(7):
+        one, two = fields[2 * g], fields[2 * g + 1]
+        even = jnp.where(low, one, pltpu.roll(two, 4, 0))
+        odd = jnp.where(low, pltpu.roll(one, 124, 0), two)
+        for m in range(16):
+            out_ref[2 * m, 8 * g : 8 * g + 8] = even[8 * m : 8 * m + 8]
+            out_ref[2 * m + 1, 8 * g : 8 * g + 8] = odd[8 * m : 8 * m + 8]
 
 
 def scatter_factors(tab_ref, i, base_col, a_ref, z_ref):
@@ -132,8 +140,8 @@
                 force = tab_ref[i, pl.ds(32 + 4 * c + s, 1)]
                 parts = []
                 for kx in range(2):
-                    w0 = tab_ref[i, pl.ds(8 * s + 4 * kx + kz, 1)] * force
-                    w1 = tab_ref[i, pl.ds(8 * s + 4 * kx + 2 + kz, 1)] * force
+                    w0 = tab_ref[i, pl.ds(4 * (4 * kx + kz) + s, 1)] * force
+                    w1 = tab_ref[i, pl.ds(4 * (4 * kx + 2 + kz) + s, 1)] * force
                     parts.append(halves(jnp.where(at_y, w0, jnp.where(at_y1, w1, 0.0))))
                 base = (kz * 3 + c) * HALF
                 for hl in range(2):
@@ -188,7 +196,11 @@
             vel_ref[a, rows] = u
         speed_sq = velocity[0] * velocity[0] + velocity[1] * velocity[1] + velocity[2] * velocity[2]
         u_dot_f = velocity[0] * force[0] + velocity[1] * force[1] + velocity[2] * force[2]
-        common = 1.0 - 1.5 * speed_sq
+        rate = density * (1.0 / RELAXATION)
+        common = rate * (1.0 - 1.5 * speed_sq) - (3.0 * factor) * u_dot_f
+        square = [4.5 * rate * velocity[a] + (9.0 * factor) * force[a] for a in range(3)]
+        linear = [3.0 * rate * velocity[a] + (3.0 * factor) * force[a] for a in range(3)]
+        keep = 1.0 - 1.0 / RELAXATION
 
         def along(direction, parts):
             total = None
@@ -198,18 +210,14 @@
                     total = term if total is None else total + term
             return total
 
-        for q in range(19):
+        relaxed = keep * pops[0] + LATTICE_WEIGHTS[0] * common
+        post_ref[0, x, yy] = jnp.where(solid, pops[0], relaxed)
+        for q in range(1, 19, 2):
             w = LATTICE_WEIGHTS[q]
-            if q == 0:
-                equilibrium = w * density * common
-                forcing = (factor * w) * (-3.0 * u_dot_f)
-            else:
-                along_u = along(VELOCITIES[q], velocity)
-                along_f = along(VELOCITIES[q], force)
-                equilibrium = w * density * (common + along_u * (3.0 + 4.5 * along_u))
-                forcing = (factor * w) * (3.0 * (along_f - u_dot_f) + 9.0 * along_u * along_f)
-            relaxed = pops[q] - (pops[q] - equilibrium) * (1.0 / RELAXATION) + forcing
-            post_ref[q, x, yy] = jnp.where(solid, pops[OPPOSITE[q]], relaxed)
+            even = w * (common + along(VELOCITIES[q], velocity) * along(VELOCITIES[q], square))
+            odd = w * along(VELOCITIES[q], linear)
+            post_ref[q, x, yy] = jnp.where(solid, pops[q + 1], keep * pops[q] + (even + odd))
+            post_ref[q + 1, x, yy] = jnp.where(solid, pops[q], keep * pops[q + 1] + (even - odd))
         return carry
 
     lax.fori_loop(0, 32, chunk, 0)
@@ -239,8 +247,8 @@
         for kz in range(2):
             parts = []
             for kx in range(2):
-                w0 = tab_ref[i, pl.ds(8 * s + 4 * kx + kz, 1)]
-                w1 = tab_ref[i, pl.ds(8 * s + 4 * kx + 2 + kz, 1)]
+                w0 = tab_ref[i, pl.ds(4 * (4 * kx + kz) + s, 1)]
+                w1 = tab_ref[i, pl.ds(4 * (4 * kx + 2 + kz) + s, 1)]
                 parts.append(halves(jnp.where(at_y, w0, jnp.where(at_y1, w1, 0.0))))
             cols = slice(kz * VERT, (kz + 1) * VERT)
             for hl in range(2):
@@ -320,14 +328,15 @@
 
 
 def step_kernel(
-    out_ref, tgt_ref, pop_hbm, solid_hbm, read_hbm, vertex_ref,
-    tab_ref, pop_ref, solid_ref, post_ref, a_ref, z_ref, acc_ref, force_ref, vel_ref, vt_ref, b_ref,
-    ret_ref, back_ref, xs_ref, xr_ref, ys_ref, yr_ref, zs_ref, zr_ref,
-    tab_send, tab_recv, ret_send, ret_recv, halo_send, halo_recv, load_sem, store_sem,
+    inter_ref, pos_ref, anc_ref, cell_ref, w_ref, pop_hbm, solid_hbm, post_ref, vertex_ref,
+    out_ref, tab_ref, pop_ref, solid_ref, a_ref, z_ref, acc_ref, force_ref, vel_ref, vt_ref, b_ref,
+    ret_ref, back_ref, xs_ref, xr_ref, ys_ref, yr_ref, zs_ref, zr_ref, pad_ref, place_ref, tgt_ref,
+    field_ref, part_ref, tab_send, tab_recv, ret_send, ret_recv, halo_send, halo_recv, load_sem,
 ):
     my_x, my_y, my_z = lax.axis_index("gx"), lax.axis_index("gy"), lax.axis_index("gz")
     load_pop = pltpu.make_async_copy(pop_hbm, pop_ref, load_sem.at[0])
     load_solid = pltpu.make_async_copy(solid_hbm, solid_ref, load_sem.at[1])
+    load_target = pltpu.make_async_copy(place_ref, tgt_ref, load_sem.at[2])
     load_pop.start()
     load_solid.start()
 
@@ -355,6 +364,9 @@
     lax.fori_loop(1, BRICKS, greet, 0)
     pl.semaphore_signal(barrier, inc=1, device_id=up_x, device_id_type=MESH)
     pl.semaphore_signal(barrier, inc=1, device_id=down_x, device_id_type=MESH)
+    slots = choose_slots(inter_ref, pad_ref, place_ref, my_y, my_z)
+    load_target.start()
+    make_tables(slots, pos_ref, anc_ref, cell_ref, w_ref, field_ref, part_ref, out_ref, my_x)
     pl.semaphore_wait(barrier, BRICKS + 1)
 
     def table_copy(i):
@@ -430,19 +442,14 @@
     halo[1].start()
     transpose_velocity(vel_ref, vt_ref)
 
-    def store_copy(q):
-        return pltpu.make_async_copy(post_ref.at[q], read_hbm.at[q], store_sem.at[q])
-
-    along_z = PLUS[2] + MINUS[2]
-
     def gather(t, carry):
         for j in range(2):
-            i = BRICKS - 1 - (2 * t + j)
-            gather_chunk(tab_ref, i, b_ref, vt_ref, ret_ref)
-
-            @pl.when(i > 0)
-            def _():
-                return_copy(i).start()
+            gather_chunk(tab_ref, BRICKS - 1 - (2 * t + j), b_ref.at[j], vt_ref, ret_ref)
+        return_copy(BRICKS - 1 - 2 * t).start()
+
+        @pl.when(t < BRICKS // 2 - 1)
+        def _():
+            return_copy(BRICKS - 2 - 2 * t).start()
 
         @pl.when(t == 3)
         def _():
@@ -460,9 +467,6 @@
             halo[2].wait_recv()
             halo[3].wait_recv()
             shift_y(post_ref, yr_ref)
-            for q in range(19):
-                if q not in along_z:
-                    store_copy(q).start()
             turn_z(post_ref, zs_ref)
             halo[4].start()
             halo[5].start()
@@ -472,8 +476,6 @@
             halo[4].wait_recv()
             halo[5].wait_recv()
             shift_z(post_ref, zr_ref)
-            for q in along_z:
-                store_copy(q).start()
 
         return carry
 
@@ -486,8 +488,11 @@
 
     lax.fori_loop(1, BRICKS, wait_return, 0)
 
+    load_target.wait()
+
     def patch(p, carry):
-        first, second = tgt_ref[0, p], tgt_ref[1, p]
+        first = jnp.clip(tgt_ref[0, p], 0, BRICKS * SLOT_CAP - 1)
+        second = jnp.clip(tgt_ref[1, p], 0, BRICKS * SLOT_CAP - 1)
         for c in range(3):
             vertex_ref[c, pl.ds(p, 1)] = (
                 back_ref[first // SLOT_CAP, pl.ds(4 * c + first % SLOT_CAP, 1)]
@@ -505,14 +510,11 @@
     lax.fori_loop(1, BRICKS, wait_sends, 0)
     for copy in halo:
         copy.wait_send()
-    for q in range(19):
-        store_copy(q).wait()
-
-
-def step(outgoing, target, populations, solid_flags):
+
+
+def step(intersection, positions, anchors, base_cell, weights, populations, solid_flags):
     vmem = pl.BlockSpec(memory_space=pltpu.VMEM)
-    smem = pl.BlockSpec(memory_space=pltpu.SMEM)
-    anywhere = pl.BlockSpec(memory_space=pl.ANY)
+    hbm = pl.BlockSpec(memory_space=pltpu.HBM)
     dma = pltpu.SemaphoreType.DMA
     return pl.pallas_call(
         step_kernel,
@@ -521,20 +523,20 @@
             jax.ShapeDtypeStruct(populations.shape, F32),
             jax.ShapeDtypeStruct((3, PATCH_DEV, VERT), F32),
         ),
-        in_specs=[vmem, smem, anywhere, anywhere],
-        out_specs=(anywhere, vmem),
+        in_specs=[vmem, vmem, vmem, vmem, vmem, hbm, hbm],
+        out_specs=(vmem, vmem),
         scratch_shapes=[
+            pltpu.VMEM((BRICKS, ROWS, VERT), F32),
             pltpu.VMEM((BRICKS, ROWS, VERT), F32),
             pltpu.VMEM((19, 16, 16, 128), F32),
             pltpu.VMEM((16, 16, 128), jnp.int32),
-            pltpu.VMEM((19, 16, 16, 128), F32),
             pltpu.VMEM((6 * HALF, 2048), BF16),
             pltpu.VMEM((256, 2048), BF16),
             pltpu.VMEM((6 * HALF, 256), F32),
             pltpu.VMEM((3, 256, 128), F32),
             pltpu.VMEM((3, 256, 128), F32),
             pltpu.VMEM((384, 768), BF16),
-            pltpu.VMEM((4, 768, 256), BF16),
+            pltpu.VMEM((2, 4, 768, 256), BF16),
             pltpu.VMEM((BRICKS, 12, VERT), F32),
             pltpu.VMEM((BRICKS, 12, VERT), F32),
             pltpu.VMEM((2, 5, 16, 128), F32),
@@ -543,30 +545,35 @@
             pltpu.VMEM((2, 5, 16, 128), F32),
             pltpu.VMEM((2, 256, 128), F32),
             pltpu.VMEM((2, 256, 128), F32),
+            pltpu.VMEM((8, 128), jnp.int32),
+            pltpu.VMEM((8, 128), jnp.int32),
+            pltpu.SMEM((8, 128), jnp.int32),
+            pltpu.VMEM((14, 32, VERT), F32),
+            pltpu.VMEM((96, 14 * VERT), BF16),
             dma((BRICKS,)),
             dma((BRICKS,)),
             dma((BRICKS,)),
             dma((BRICKS,)),
             dma((6,)),
             dma((6,)),
-            dma((2,)),
-            dma((19,)),
+            dma((3,)),
         ],
         compiler_params=pltpu.CompilerParams(
-            collective_id=0, has_side_effects=True, vmem_limit_bytes=40 * 1024 * 1024
+            collective_id=0, has_side_effects=True, vmem_limit_bytes=60 * 1024 * 1024
         ),
-    )(outgoing, target, populations, solid_flags)
+    )(intersection, positions, anchors, base_cell, weights, populations, solid_flags)
 
 
 def body(populations, solid_flags, positions, anchors, base_cell, weights, intersection):
-    outgoing, target = prep(
+    read, vertex = step(
         intersection.T,
         jnp.transpose(positions, (1, 0, 2)),
         jnp.transpose(anchors, (1, 0, 2)),
         jnp.transpose(base_cell, (1, 0, 2)),
         weights,
+        populations,
+        solid_flags,
     )
-    read, vertex = step(outgoing, target, populations, solid_flags)
     return (read, jnp.transpose(vertex, (1, 0, 2)))
 
 

time: 93.1 us -> 79.5 us (0.85)
  Pallas kernels: 85.7 us -> 74.7 us
  local copies, waits for them, and re-layouts: 6.53 us -> 4.01 us
    pallas_call x1, Pallas kernels: 82.2 us -> 74.7 us  [step(): pl.pallas_call(step_kernel, name='step', out_shape=(jax.ShapeDtypeStruct(...]
    pallas_call x1 -> x0, Pallas kernels: 3.46 us -> none  [prep(): pl.pallas_call(prep_kernel, name='prep', out_shape=(jax.ShapeDtypeStruct(...]
    unnamed x10 -> x4, local copies, waits for them, and re-layouts: 6.53 us -> 4.01 us
where the time goes in v3:
time: 79.5 us; the launch traced here: 79.4 us
  Pallas kernels  74.7 us (94%)
  local copies, waits for them, and re-layouts  4.01 us (5%)
    pallas_call x1, Pallas kernels, step(): pl.pallas_call(step_kernel, name='step', out_shape=(jax.ShapeDtypeStruct(...  74.7 us
    unnamed x4, local copies, waits for them, and re-layouts  4.01 us

profile of v3, /device:TPU:1, one launch (start us, length us, event | category | flops | bytes accessed | tf_op | source)
XLA Modules:
  0.0 79.4 jit_solution(4738771062414836710)
XLA Ops:
  0.6 74.7 %step.1 = (f32[19,16,16,128]{3,2,1,0:T(8,128)}, f32[3,28,128]{2,1,0:T(8,128)}) custom-call(s32[2,28]{1,0:T(2,128)} %bitcast.9, f32[3,28,128]{2,1,0:T(8,128)} %bitcast.6, f32[3,28,128]{2,1,0:T(8,128)} %bitcast.7, s32[3,28,128]{2,1,0:T(8,128)} %bitcast.8, f32[28,8,128]{2,1,0:T(8,128)} %w_ref.1, f32[19,16,16,128]{3,2,1,0:T(8,128)} %pop_hbm.1, ...), custom_call_target="tpu_custom_call" | custom-call | tf_op jit(solution)/shard_map/step/pallas_call | solution.py:519
  75.3 0.0 copy-start
  75.4 3.4 %copy.11 = f32[19,16,16,128]{3,2,1,0:T(8,128)} copy(f32[19,16,16,128]{3,2,1,0:T(8,128)} %get-tuple-element.8) | data formatting | bytes 4980736
  78.7 0.0 copy-done
  78.7 0.6 copy.12
Async XLA Ops:
  75.3 3.4 %copy-start = (f32[3,28,128]{2,1,0:T(8,128)S(1)}, f32[3,28,128]{2,1,0:T(8,128)}, u32[]{:S(2)}) copy-start(f32[3,28,128]{2,1,0:T(8,128)} %get-tuple-element.5) | copy-start | bytes 129028

commit v4 on v3

--- a/solution.py
+++ b/solution.py
@@ -39,12 +39,20 @@
 LATTICE_WEIGHTS = [1.0 / 3.0] + [1.0 / 18.0] * 6 + [1.0 / 36.0] * 12
 F32 = jnp.float32
 BF16 = jnp.bfloat16
+F8 = jnp.float8_e4m3fn
+LOW_SCALE = 4096.0
+TOP = 24.0
 OUTSIDE = -100.0
 
 
+def split(value):
+    high = value.astype(BF16)
+    return high, value - high.astype(F32)
+
+
 def halves(value):
-    high = value.astype(BF16)
-    return high, (value - high.astype(F32)).astype(BF16)
+    high, low = split(value)
+    return high, low.astype(BF16)
 
 
 def thirds(value):
@@ -186,7 +194,7 @@
         force = [force_ref[c, rows] for c in range(3)]
         density = sum(pops[1:], pops[0])
         inverse = 1.0 / density
-        velocity = []
+        velocity, largest = [], carry
         for a in range(3):
             plus = [pops[q] for q in range(19) if VELOCITIES[q][a] == 1]
             minus = [pops[q] for q in range(19) if VELOCITIES[q][a] == -1]
@@ -194,6 +202,7 @@
             u = (momentum + 0.5 * force[a]) * inverse
             velocity.append(u)
             vel_ref[a, rows] = u
+            largest = jnp.maximum(largest, jnp.abs(u))
         speed_sq = velocity[0] * velocity[0] + velocity[1] * velocity[1] + velocity[2] * velocity[2]
         u_dot_f = velocity[0] * force[0] + velocity[1] * force[1] + velocity[2] * force[2]
         rate = density * (1.0 / RELAXATION)
@@ -218,21 +227,24 @@
             odd = w * along(VELOCITIES[q], linear)
             post_ref[q, x, yy] = jnp.where(solid, pops[q + 1], keep * pops[q] + (even + odd))
             post_ref[q + 1, x, yy] = jnp.where(solid, pops[q], keep * pops[q + 1] + (even - odd))
-        return carry
-
-    lax.fori_loop(0, 32, chunk, 0)
-
-
-def transpose_velocity(vel_ref, vt_ref):
+        return largest
+
+    return lax.fori_loop(0, 32, chunk, jnp.zeros((8, 128), F32))
+
+
+def transpose_velocity(vel_ref, largest, vt_ref, vt8_ref):
+    largest = jnp.maximum(jnp.max(jnp.max(largest, axis=0, keepdims=True), axis=1, keepdims=True), 1e-30)
+    scale = TOP / largest
     for c in range(3):
-        high, low = halves(vel_ref[c].T)
+        high, low = split(vel_ref[c].T)
         rows = slice(c * 128, (c + 1) * 128)
-        vt_ref[rows, 0:256] = high
-        vt_ref[rows, 256:512] = high
-        vt_ref[rows, 512:768] = low
-
-
-def gather_chunk(tab_ref, i, b_ref, vt_ref, ret_ref):
+        vt_ref[rows] = high
+        vt8_ref[rows, 0:256] = (high.astype(F32) * scale).astype(F8)
+        vt8_ref[rows, 256:512] = (low * (scale * LOW_SCALE)).astype(F8)
+    return largest * (1.0 / (TOP * LOW_SCALE))
+
+
+def gather_chunk(tab_ref, i, b_ref, b8_ref, vt_ref, vt8_ref, undo, ret_ref):
     y_iota = lax.broadcasted_iota(jnp.int32, (16, VERT), 0).astype(F32)
     z_iota = lax.broadcasted_iota(jnp.int32, (VERT, VERT), 0).astype(F32)
     zero16 = jnp.zeros((16, VERT), BF16)
@@ -249,20 +261,27 @@
             for kx in range(2):
                 w0 = tab_ref[i, pl.ds(4 * (4 * kx + kz) + s, 1)]
                 w1 = tab_ref[i, pl.ds(4 * (4 * kx + 2 + kz) + s, 1)]
-                parts.append(halves(jnp.where(at_y, w0, jnp.where(at_y1, w1, 0.0))))
+                high, low = split(jnp.where(at_y, w0, jnp.where(at_y1, w1, 0.0)))
+                parts.append((high, (low * LOW_SCALE).astype(BF16)))
             cols = slice(kz * VERT, (kz + 1) * VERT)
             for hl in range(2):
-                for plane in range(16):
-                    value = jnp.where(
-                        masks[plane + 1],
-                        parts[0][hl],
-                        jnp.where(masks[plane], parts[1][hl], zero16),
-                    )
-                    row = hl * 256 + plane * 16
-                    b_ref[s, row : row + 16, cols] = value
+                for pair in range(8):
+                    planes = [
+                        jnp.where(
+                            masks[plane + 1],
+                            parts[0][hl],
+                            jnp.where(masks[plane], parts[1][hl], zero16),
+                        )
+                        for plane in (2 * pair, 2 * pair + 1)
+                    ]
+                    both = jnp.concatenate(planes, axis=0)
+                    row = pair * 32
                     if hl == 0:
-                        b_ref[s, 512 + plane * 16 : 528 + plane * 16, cols] = value
+                        b_ref[s, row : row + 32, cols] = both
+                    row = row + 256 * (1 - hl)
+                    b8_ref[s, row : row + 32, cols] = both.astype(F8)
         picked = jnp.dot(vt_ref[...], b_ref[s], preferred_element_type=F32)
+        picked = picked + undo * jnp.dot(vt8_ref[...], b8_ref[s], preferred_element_type=F32)
         at_z = z_iota == z
         at_z1 = z_iota - 1.0 == z
         for c in range(3):
@@ -329,7 +348,7 @@
 
 def step_kernel(
     inter_ref, pos_ref, anc_ref, cell_ref, w_ref, pop_hbm, solid_hbm, post_ref, vertex_ref,
-    out_ref, tab_ref, pop_ref, solid_ref, a_ref, z_ref, acc_ref, force_ref, vel_ref, vt_ref, b_ref,
+    out_ref, tab_ref, pop_ref, solid_ref, a_ref, z_ref, acc_ref, force_ref, vel_ref, vt_ref, vt8_ref, b_ref, b8_ref,
     ret_ref, back_ref, xs_ref, xr_ref, ys_ref, yr_ref, zs_ref, zr_ref, pad_ref, place_ref, tgt_ref,
     field_ref, part_ref, tab_send, tab_recv, ret_send, ret_recv, halo_send, halo_recv, load_sem,
 ):
@@ -415,7 +434,7 @@
     finish_force(acc_ref, force_ref)
     load_pop.wait()
     load_solid.wait()
-    collide_all(pop_ref, solid_ref, force_ref, post_ref, vel_ref)
+    largest = collide_all(pop_ref, solid_ref, force_ref, post_ref, vel_ref)
 
     def halo_copy(k, src, dst, to):
         return pltpu.make_async_remote_copy(
@@ -440,11 +459,12 @@
         xs_ref[1, k] = post_ref[MINUS[0][k], 0]
     halo[0].start()
     halo[1].start()
-    transpose_velocity(vel_ref, vt_ref)
+    undo = transpose_velocity(vel_ref, largest, vt_ref, vt8_ref)
 
     def gather(t, carry):
         for j in range(2):
-            gather_chunk(tab_ref, BRICKS - 1 - (2 * t + j), b_ref.at[j], vt_ref, ret_ref)
+            i = BRICKS - 1 - (2 * t + j)
+            gather_chunk(tab_ref, i, b_ref.at[j], b8_ref.at[j], vt_ref, vt8_ref, undo, ret_ref)
         return_copy(BRICKS - 1 - 2 * t).start()
 
         @pl.when(t < BRICKS // 2 - 1)
@@ -535,8 +555,10 @@
             pltpu.VMEM((6 * HALF, 256), F32),
             pltpu.VMEM((3, 256, 128), F32),
             pltpu.VMEM((3, 256, 128), F32),
-            pltpu.VMEM((384, 768), BF16),
-            pltpu.VMEM((2, 4, 768, 256), BF16),
+            pltpu.VMEM((384, 256), BF16),
+            pltpu.VMEM((384, 512), F8),
+            pltpu.VMEM((2, 4, 256, 256), BF16),
+            pltpu.VMEM((2, 4, 512, 256), F8),
             pltpu.VMEM((BRICKS, 12, VERT), F32),
             pltpu.VMEM((BRICKS, 12, VERT), F32),
             pltpu.VMEM((2, 5, 16, 128), F32),

time: 79.5 us -> 76 us (0.956)
  Pallas kernels: 74.7 us -> 71.3 us
    pallas_call x1, Pallas kernels: 74.7 us -> 71.3 us  [step(): pl.pallas_call(step_kernel, name='step', out_shape=(jax.ShapeDtypeStruct(...]
where the time goes in v4:
time: 76 us; the launch traced here: 75.9 us
  Pallas kernels  71.3 us (94%)
  local copies, waits for them, and re-layouts  4.01 us (5%)
    pallas_call x1, Pallas kernels, step(): pl.pallas_call(step_kernel, name='step', out_shape=(jax.ShapeDtypeStruct(...  71.3 us
    unnamed x4, local copies, waits for them, and re-layouts  4.01 us

profile of v4, /device:TPU:1, one launch (start us, length us, event | category | flops | bytes accessed | tf_op | source)
XLA Modules:
  0.0 75.9 jit_solution(2143943129455117500)
XLA Ops:
  0.6 71.3 %step.1 = (f32[19,16,16,128]{3,2,1,0:T(8,128)}, f32[3,28,128]{2,1,0:T(8,128)}) custom-call(s32[2,28]{1,0:T(2,128)} %bitcast.9, f32[3,28,128]{2,1,0:T(8,128)} %bitcast.6, f32[3,28,128]{2,1,0:T(8,128)} %bitcast.7, s32[3,28,128]{2,1,0:T(8,128)} %bitcast.8, f32[28,8,128]{2,1,0:T(8,128)} %w_ref.1, f32[19,16,16,128]{3,2,1,0:T(8,128)} %pop_hbm.1, ...), custom_call_target="tpu_custom_call" | custom-call | tf_op jit(solution)/shard_map/step/pallas_call | solution.py:539
  71.9 0.0 copy-start
  71.9 3.4 %copy.11 = f32[19,16,16,128]{3,2,1,0:T(8,128)} copy(f32[19,16,16,128]{3,2,1,0:T(8,128)} %get-tuple-element.8) | data formatting | bytes 4980736
  75.3 0.0 copy-done
  75.3 0.6 copy.12
Async XLA Ops:
  71.9 3.4 %copy-start = (f32[3,28,128]{2,1,0:T(8,128)S(1)}, f32[3,28,128]{2,1,0:T(8,128)}, u32[]{:S(2)}) copy-start(f32[3,28,128]{2,1,0:T(8,128)} %get-tuple-element.5) | copy-start | bytes 129028

commit v5 on v4

--- a/solution.py
+++ b/solution.py
@@ -48,11 +48,6 @@
 def split(value):
     high = value.astype(BF16)
     return high, value - high.astype(F32)
-
-
-def halves(value):
-    high, low = split(value)
-    return high, low.astype(BF16)
 
 
 def thirds(value):
@@ -125,10 +120,12 @@
             out_ref[2 * m + 1, 8 * g : 8 * g + 8] = odd[8 * m : 8 * m + 8]
 
 
-def scatter_factors(tab_ref, i, base_col, a_ref, z_ref):
+def scatter_factors(tab_ref, i, base_col, a_ref, a8_ref, z_ref, z8_ref):
     y_iota = lax.broadcasted_iota(jnp.int32, (16, VERT), 0).astype(F32)
-    z_iota = lax.broadcasted_iota(jnp.int32, (256, VERT), 0).astype(F32)
+    z_iota = lax.broadcasted_iota(jnp.int32, (256, VERT), 0).astype(F32).astype(BF16)
     zero16 = jnp.zeros((16, VERT), BF16)
+    ones = jnp.ones((256, VERT), BF16)
+    zeros = jnp.zeros((256, VERT), BF16)
     for s in range(SLOT_CAP):
         x = tab_ref[i, pl.ds(44 + s, 1)]
         y = tab_ref[i, pl.ds(48 + s, 1)]
@@ -136,30 +133,42 @@
         upper = x >= 8.0
         x_in = jnp.where(upper, x - 8.0, x)
         column = jnp.where(upper, z + 128.0, z)
-        hot = jnp.where(z_iota == column, 1.0, 0.0).astype(BF16)
-        for hl in range(2):
-            z_ref[:, pl.ds(base_col + hl * 512 + s * VERT, VERT)] = hot
+        col = slice(base_col + s * VERT, base_col + (s + 1) * VERT)
+        hot = jnp.where(
+            z_iota == jnp.broadcast_to(column, (256, VERT)).astype(BF16), ones, zeros
+        )
+        z_ref[:, col] = hot
+        z8_ref[:, col] = hot.astype(F8)
         at_y = y_iota == y
         at_y1 = y_iota - 1.0 == y
         x_wide = jnp.broadcast_to(x_in, (16, VERT)).astype(BF16)
         masks = [x_wide == jnp.asarray(k, BF16) for k in range(-1, 9)]
-        for kz in range(2):
-            for c in range(3):
+        for pair in range(3):
+            blocks = []
+            for kz, c in (divmod(2 * pair, 3), divmod(2 * pair + 1, 3)):
                 force = tab_ref[i, pl.ds(32 + 4 * c + s, 1)]
                 parts = []
                 for kx in range(2):
                     w0 = tab_ref[i, pl.ds(4 * (4 * kx + kz) + s, 1)] * force
                     w1 = tab_ref[i, pl.ds(4 * (4 * kx + 2 + kz) + s, 1)] * force
-                    parts.append(halves(jnp.where(at_y, w0, jnp.where(at_y1, w1, 0.0))))
-                base = (kz * 3 + c) * HALF
-                for hl in range(2):
-                    col = pl.ds(base_col + hl * 512 + s * VERT, VERT)
-                    for plane in range(9):
-                        a_ref[base + plane * 16 : base + plane * 16 + 16, col] = jnp.where(
-                            masks[plane + 1],
-                            parts[0][hl],
-                            jnp.where(masks[plane], parts[1][hl], zero16),
-                        )
+                    high, low = split(jnp.where(at_y, w0, jnp.where(at_y1, w1, 0.0)))
+                    parts.append((high, (low * LOW_SCALE).astype(BF16)))
+                for plane in range(9):
+                    blocks.append(
+                        [
+                            jnp.where(
+                                masks[plane + 1],
+                                parts[0][hl],
+                                jnp.where(masks[plane], parts[1][hl], zero16),
+                            )
+                            for hl in range(2)
+                        ]
+                    )
+            for n in range(9):
+                rows = slice(pair * 2 * HALF + n * 32, pair * 2 * HALF + n * 32 + 32)
+                first, second = blocks[2 * n], blocks[2 * n + 1]
+                a_ref[rows, col] = jnp.concatenate([first[0], second[0]], axis=0)
+                a8_ref[rows, col] = jnp.concatenate([first[1], second[1]], axis=0).astype(F8)
 
 
 def finish_force(acc_ref, force_ref):
@@ -347,10 +356,10 @@
 
 
 def step_kernel(
-    inter_ref, pos_ref, anc_ref, cell_ref, w_ref, pop_hbm, solid_hbm, post_ref, vertex_ref,
-    out_ref, tab_ref, pop_ref, solid_ref, a_ref, z_ref, acc_ref, force_ref, vel_ref, vt_ref, vt8_ref, b_ref, b8_ref,
+    inter_ref, pos_ref, anc_ref, cell_ref, w_ref, pop_hbm, solid_hbm, read_hbm, vertex_ref,
+    out_ref, tab_ref, pop_ref, solid_ref, post_ref, a_ref, a8_ref, z_ref, z8_ref, acc_ref, force_ref, vel_ref, vt_ref, vt8_ref, b_ref, b8_ref,
     ret_ref, back_ref, xs_ref, xr_ref, ys_ref, yr_ref, zs_ref, zr_ref, pad_ref, place_ref, tgt_ref,
-    field_ref, part_ref, tab_send, tab_recv, ret_send, ret_recv, halo_send, halo_recv, load_sem,
+    field_ref, part_ref, tab_send, tab_recv, ret_send, ret_recv, halo_send, halo_recv, load_sem, store_sem,
 ):
     my_x, my_y, my_z = lax.axis_index("gx"), lax.axis_index("gy"), lax.axis_index("gz")
     load_pop = pltpu.make_async_copy(pop_hbm, pop_ref, load_sem.at[0])
@@ -424,10 +433,11 @@
 
         table_copy(2 * t + 1).wait_recv()
         for j in range(2):
-            scatter_factors(tab_ref, 2 * t + j, j * 1024, a_ref, z_ref)
-        acc_ref[...] += lax.dot_general(
-            a_ref[...], z_ref[...], (((1,), (1,)), ((), ())), preferred_element_type=F32
-        )
+            scatter_factors(tab_ref, 2 * t + j, j * 512, a_ref, a8_ref, z_ref, z8_ref)
+        dims = (((1,), (1,)), ((), ()))
+        high = lax.dot_general(a_ref[...], z_ref[...], dims, preferred_element_type=F32)
+        low = lax.dot_general(a8_ref[...], z8_ref[...], dims, preferred_element_type=F32)
+        acc_ref[...] += high + low * (1.0 / LOW_SCALE)
         return carry
 
     lax.fori_loop(0, BRICKS // 2, scatter, 0)
@@ -461,6 +471,11 @@
     halo[1].start()
     undo = transpose_velocity(vel_ref, largest, vt_ref, vt8_ref)
 
+    def store_copy(q):
+        return pltpu.make_async_copy(post_ref.at[q], read_hbm.at[q], store_sem.at[q])
+
+    along_z = PLUS[2] + MINUS[2]
+
     def gather(t, carry):
         for j in range(2):
             i = BRICKS - 1 - (2 * t + j)
@@ -487,6 +502,9 @@
             halo[2].wait_recv()
             halo[3].wait_recv()
             shift_y(post_ref, yr_ref)
+            for q in range(19):
+                if q not in along_z:
+                    store_copy(q).start()
             turn_z(post_ref, zs_ref)
             halo[4].start()
             halo[5].start()
@@ -496,6 +514,8 @@
             halo[4].wait_recv()
             halo[5].wait_recv()
             shift_z(post_ref, zr_ref)
+            for q in along_z:
+                store_copy(q).start()
 
         return carry
 
@@ -530,6 +550,8 @@
     lax.fori_loop(1, BRICKS, wait_sends, 0)
     for copy in halo:
         copy.wait_send()
+    for q in range(19):
+        store_copy(q).wait()
 
 
 def step(intersection, positions, anchors, base_cell, weights, populations, solid_flags):
@@ -544,14 +566,17 @@
             jax.ShapeDtypeStruct((3, PATCH_DEV, VERT), F32),
         ),
         in_specs=[vmem, vmem, vmem, vmem, vmem, hbm, hbm],
-        out_specs=(vmem, vmem),
+        out_specs=(hbm, vmem),
         scratch_shapes=[
             pltpu.VMEM((BRICKS, ROWS, VERT), F32),
             pltpu.VMEM((BRICKS, ROWS, VERT), F32),
             pltpu.VMEM((19, 16, 16, 128), F32),
             pltpu.VMEM((16, 16, 128), jnp.int32),
-            pltpu.VMEM((6 * HALF, 2048), BF16),
-            pltpu.VMEM((256, 2048), BF16),
+            pltpu.VMEM((19, 16, 16, 128), F32),
+            pltpu.VMEM((6 * HALF, 1024), BF16),
+            pltpu.VMEM((6 * HALF, 1024), F8),
+            pltpu.VMEM((256, 1024), BF16),
+            pltpu.VMEM((256, 1024), F8),
             pltpu.VMEM((6 * HALF, 256), F32),
             pltpu.VMEM((3, 256, 128), F32),
             pltpu.VMEM((3, 256, 128), F32),
@@ -579,6 +604,7 @@
             dma((6,)),
             dma((6,)),
             dma((3,)),
+            dma((19,)),
         ],
         compiler_params=pltpu.CompilerParams(
             collective_id=0, has_side_effects=True, vmem_limit_bytes=60 * 1024 * 1024

time: 76 us -> 71.7 us (0.943)
  Pallas kernels: 71.3 us -> 66.9 us
    pallas_call x1, Pallas kernels: 71.3 us -> 66.9 us  [step(): pl.pallas_call(step_kernel, name='step', out_shape=(jax.ShapeDtypeStruct(...]
where the time goes in v5:
time: 71.7 us; the launch traced here: 71.6 us
  Pallas kernels  66.9 us (93%)
  local copies, waits for them, and re-layouts  4.01 us (6%)
    pallas_call x1, Pallas kernels, step(): pl.pallas_call(step_kernel, name='step', out_shape=(jax.ShapeDtypeStruct(...  66.9 us
    unnamed x4, local copies, waits for them, and re-layouts  4.01 us

profile of v5, /device:TPU:1, one launch (start us, length us, event | category | flops | bytes accessed | tf_op | source)
XLA Modules:
  0.0 71.6 jit_solution(6367587372737904685)
XLA Ops:
  0.6 66.9 %step.1 = (f32[19,16,16,128]{3,2,1,0:T(8,128)}, f32[3,28,128]{2,1,0:T(8,128)}) custom-call(s32[2,28]{1,0:T(2,128)} %bitcast.9, f32[3,28,128]{2,1,0:T(8,128)} %bitcast.6, f32[3,28,128]{2,1,0:T(8,128)} %bitcast.7, s32[3,28,128]{2,1,0:T(8,128)} %bitcast.8, f32[28,8,128]{2,1,0:T(8,128)} %w_ref.1, f32[19,16,16,128]{3,2,1,0:T(8,128)} %pop_hbm.1, ...), custom_call_target="tpu_custom_call" | custom-call | tf_op jit(solution)/shard_map/step/pallas_call | solution.py:561
  67.6 0.0 copy-start
  67.6 3.4 %copy.11 = f32[19,16,16,128]{3,2,1,0:T(8,128)} copy(f32[19,16,16,128]{3,2,1,0:T(8,128)} %get-tuple-element.8) | data formatting | bytes 4980736
  71.0 0.0 copy-done
  71.0 0.6 copy.12
Async XLA Ops:
  67.6 3.4 %copy-start = (f32[3,28,128]{2,1,0:T(8,128)S(1)}, f32[3,28,128]{2,1,0:T(8,128)}, u32[]{:S(2)}) copy-start(f32[3,28,128]{2,1,0:T(8,128)} %get-tuple-element.5) | copy-start | bytes 129028

commit v6 on v5

--- a/solution.py
+++ b/solution.py
@@ -238,7 +238,7 @@
             post_ref[q + 1, x, yy] = jnp.where(solid, pops[q], keep * pops[q + 1] + (even - odd))
         return largest
 
-    return lax.fori_loop(0, 32, chunk, jnp.zeros((8, 128), F32))
+    return lax.fori_loop(0, 32, chunk, jnp.zeros((8, 128), F32), unroll=2)
 
 
 def transpose_velocity(vel_ref, largest, vt_ref, vt8_ref):
@@ -477,16 +477,17 @@
     along_z = PLUS[2] + MINUS[2]
 
     def gather(t, carry):
-        for j in range(2):
-            i = BRICKS - 1 - (2 * t + j)
+        for j in range(4):
+            i = BRICKS - 1 - (4 * t + j)
             gather_chunk(tab_ref, i, b_ref.at[j], b8_ref.at[j], vt_ref, vt8_ref, undo, ret_ref)
-        return_copy(BRICKS - 1 - 2 * t).start()
-
-        @pl.when(t < BRICKS // 2 - 1)
+        for j in range(3):
+            return_copy(BRICKS - 1 - (4 * t + j)).start()
+
+        @pl.when(t < BRICKS // 4 - 1)
         def _():
-            return_copy(BRICKS - 2 - 2 * t).start()
-
-        @pl.when(t == 3)
+            return_copy(BRICKS - 4 - 4 * t).start()
+
+        @pl.when(t == 1)
         def _():
             halo[0].wait_recv()
             halo[1].wait_recv()
@@ -497,7 +498,7 @@
             halo[2].start()
             halo[3].start()
 
-        @pl.when(t == 7)
+        @pl.when(t == 3)
         def _():
             halo[2].wait_recv()
             halo[3].wait_recv()
@@ -509,7 +510,7 @@
             halo[4].start()
             halo[5].start()
 
-        @pl.when(t == 11)
+        @pl.when(t == 5)
         def _():
             halo[4].wait_recv()
             halo[5].wait_recv()
@@ -519,11 +520,13 @@
 
         return carry
 
-    lax.fori_loop(0, BRICKS // 2, gather, 0)
+    lax.fori_loop(0, BRICKS // 4, gather, 0)
     back_ref[0] = ret_ref[0]
 
     def wait_return(i, carry):
         return_copy(i).wait_recv()
+        return_copy(i).wait_send()
+        table_copy(i).wait_send()
         return carry
 
     lax.fori_loop(1, BRICKS, wait_return, 0)
@@ -540,14 +543,8 @@
             )
         return carry
 
-    lax.fori_loop(0, PATCH_DEV, patch, 0)
-
-    def wait_sends(i, carry):
-        table_copy(i).wait_send()
-        return_copy(i).wait_send()
-        return carry
-
-    lax.fori_loop(1, BRICKS, wait_sends, 0)
+    lax.fori_loop(0, PATCH_DEV, patch, 0, unroll=4)
+
     for copy in halo:
         copy.wait_send()
     for q in range(19):
@@ -582,8 +579,8 @@
             pltpu.VMEM((3, 256, 128), F32),
             pltpu.VMEM((384, 256), BF16),
             pltpu.VMEM((384, 512), F8),
-            pltpu.VMEM((2, 4, 256, 256), BF16),
-            pltpu.VMEM((2, 4, 512, 256), F8),
+            pltpu.VMEM((4, 4, 256, 256), BF16),
+            pltpu.VMEM((4, 4, 512, 256), F8),
             pltpu.VMEM((BRICKS, 12, VERT), F32),
             pltpu.VMEM((BRICKS, 12, VERT), F32),
             pltpu.VMEM((2, 5, 16, 128), F32),

time: 71.7 us -> 70.9 us (0.989)
    pallas_call x1, Pallas kernels: 66.9 us -> 66.2 us  [step(): pl.pallas_call(step_kernel, name='step', out_shape=(jax.ShapeDtypeStruct(...]
where the time goes in v6:
time: 70.9 us; the launch traced here: 70.8 us
  Pallas kernels  66.2 us (93%)
  local copies, waits for them, and re-layouts  4.01 us (6%)
    pallas_call x1, Pallas kernels, step(): pl.pallas_call(step_kernel, name='step', out_shape=(jax.ShapeDtypeStruct(...  66.2 us
    unnamed x4, local copies, waits for them, and re-layouts  4.01 us

profile of v6, /device:TPU:1, one launch (start us, length us, event | category | flops | bytes accessed | tf_op | source)
XLA Modules:
  0.0 70.8 jit_solution(3856289988399960903)
XLA Ops:
  0.6 66.2 %step.1 = (f32[19,16,16,128]{3,2,1,0:T(8,128)}, f32[3,28,128]{2,1,0:T(8,128)}) custom-call(s32[2,28]{1,0:T(2,128)} %bitcast.9, f32[3,28,128]{2,1,0:T(8,128)} %bitcast.6, f32[3,28,128]{2,1,0:T(8,128)} %bitcast.7, s32[3,28,128]{2,1,0:T(8,128)} %bitcast.8, f32[28,8,128]{2,1,0:T(8,128)} %w_ref.1, f32[19,16,16,128]{3,2,1,0:T(8,128)} %pop_hbm.1, ...), custom_call_target="tpu_custom_call" | custom-call | tf_op jit(solution)/shard_map/step/pallas_call | solution.py:558
  66.8 0.0 copy-start
  66.8 3.4 %copy.11 = f32[19,16,16,128]{3,2,1,0:T(8,128)} copy(f32[19,16,16,128]{3,2,1,0:T(8,128)} %get-tuple-element.8) | data formatting | bytes 4980736
  70.2 0.0 copy-done
  70.2 0.6 copy.12
Async XLA Ops:
  66.8 3.4 %copy-start = (f32[3,28,128]{2,1,0:T(8,128)S(1)}, f32[3,28,128]{2,1,0:T(8,128)}, u32[]{:S(2)}) copy-start(f32[3,28,128]{2,1,0:T(8,128)} %get-tuple-element.5) | copy-start | bytes 129028

commit v7 on v6

--- a/solution.py
+++ b/solution.py
@@ -609,6 +609,41 @@
     )(intersection, positions, anchors, base_cell, weights, populations, solid_flags)
 
 
+def place_kernel(read_in, vertex_in, read_out, vertex_out, held, vertex_held, in_sem, out_sem):
+    arrive = [pltpu.make_async_copy(read_in.at[q], held.at[q], in_sem.at[q]) for q in range(19)]
+    leave = [pltpu.make_async_copy(held.at[q], read_out.at[q], out_sem.at[q]) for q in range(19)]
+    arrive.append(pltpu.make_async_copy(vertex_in, vertex_held, in_sem.at[19]))
+    leave.append(pltpu.make_async_copy(vertex_held, vertex_out, out_sem.at[19]))
+    for copy in arrive:
+        copy.start()
+    for came, goes in zip(arrive, leave):
+        came.wait()
+        goes.start()
+    for copy in leave:
+        copy.wait()
+
+
+def place(read, vertex):
+    hbm = pl.BlockSpec(memory_space=pltpu.HBM)
+    return pl.pallas_call(
+        place_kernel,
+        name="place",
+        out_shape=(
+            jax.ShapeDtypeStruct(read.shape, F32),
+            jax.ShapeDtypeStruct(vertex.shape, F32),
+        ),
+        in_specs=[hbm, hbm],
+        out_specs=(hbm, hbm),
+        scratch_shapes=[
+            pltpu.VMEM(read.shape, F32),
+            pltpu.VMEM(vertex.shape, F32),
+            pltpu.SemaphoreType.DMA((20,)),
+            pltpu.SemaphoreType.DMA((20,)),
+        ],
+        compiler_params=pltpu.CompilerParams(vmem_limit_bytes=60 * 1024 * 1024),
+    )(read, vertex)
+
+
 def body(populations, solid_flags, positions, anchors, base_cell, weights, intersection):
     read, vertex = step(
         intersection.T,
@@ -619,6 +654,7 @@
         populations,
         solid_flags,
     )
+    read, vertex = place(read, vertex)
     return (read, jnp.transpose(vertex, (1, 0, 2)))
 
 

time: 70.9 us -> 69.7 us (0.983)
  local copies, waits for them, and re-layouts: 4.01 us -> 0 us
  Pallas kernels: 66.2 us -> 68.9 us
    unnamed x4 -> x0, local copies, waits for them, and re-layouts: 4.01 us -> none
    pallas_call x0 -> x1, Pallas kernels: none -> 2.78 us  [place(): pl.pallas_call(place_kernel, name='place', out_shape=(jax.ShapeDtypeStruc...]
where the time goes in v7:
time: 69.7 us; the launch traced here: 69.6 us
  Pallas kernels  68.9 us (99%)
    pallas_call x1, Pallas kernels, step(): pl.pallas_call(step_kernel, name='step', out_shape=(jax.ShapeDtypeStruct(...  66.2 us
    pallas_call x1, Pallas kernels, place(): pl.pallas_call(place_kernel, name='place', out_shape=(jax.ShapeDtypeStruc...  2.78 us

profile of v7, /device:TPU:1, one launch (start us, length us, event | category | flops | bytes accessed | tf_op | source)
XLA Modules:
  0.0 69.6 jit_solution(10974789292418693331)
XLA Ops:
  0.6 66.2 %step.1 = (f32[19,16,16,128]{3,2,1,0:T(8,128)}, f32[3,28,128]{2,1,0:T(8,128)}) custom-call(s32[2,28]{1,0:T(2,128)} %bitcast.8, f32[3,28,128]{2,1,0:T(8,128)} %bitcast.5, f32[3,28,128]{2,1,0:T(8,128)} %bitcast.6, s32[3,28,128]{2,1,0:T(8,128)} %bitcast.7, f32[28,8,128]{2,1,0:T(8,128)} %w_ref.1, f32[19,16,16,128]{3,2,1,0:T(8,128)} %pop_hbm.1, ...), custom_call_target="tpu_custom_call" | custom-call | tf_op jit(solution)/shard_map/step/pallas_call | solution.py:558
  66.8 2.8 %place.1 = (f32[19,16,16,128]{3,2,1,0:T(8,128)}, f32[3,28,128]{2,1,0:T(8,128)}) custom-call(f32[19,16,16,128]{3,2,1,0:T(8,128)} %get-tuple-element.6.read_in, f32[3,28,128]{2,1,0:T(8,128)} %get-tuple-element.7.vertex_in), custom_call_target="tpu_custom_call" | custom-call | tf_op jit(solution)/shard_map/place/pallas_call | solution.py:628
